TPU v7x, 512 devices: a whole 4x4x16 slice. The times are simulated.
512 devices in a mesh: lat: 64 (over x, z), sec: 8 (over y, core).
Axes of the slice: x: 4, y: 4, z: 16, core: 2. Of those that a mesh axis runs over, the one named last changes fastest.
Arguments:
- velocity: float32 [256, 64, 1024], P('lat', 'sec'), may hold values from -3 to 3
- base_visc: float32 [256, 64, 1024], P('lat', 'sec'), may hold values from 0.5 to 5
- yielded: int32 [256, 64, 1024], P('lat', 'sec'), may hold values 0 or 1
- colors: int32 [256, 64, 1024], P('lat', 'sec'), may hold values from 0 to 7, as said below
- forcing: float32 [256, 64, 1024], P('lat', 'sec'), may hold values from -6 to 6
- block_diag: float32 [2, 128, 128], replicated, may hold values from -0.0625 to 0.0625
- block_below: float32 [2, 128, 128], replicated, may hold values from -0.0625 to 0.0625
- block_above: float32 [2, 128, 128], replicated, may hold values from -0.0625 to 0.0625
- weak_lines: int32 [8, 64, 64], P('sec', 'lat'), may hold values from 0 to 127, as said below
- weak_owner: int32 [8, 64, 64, 1], P('sec', 'lat'), may hold values from 0 to 63; in each aligned block of 64 rows (0 to 63, 64 to 127, ..., all dimensions but the last counted through in order) at most 4 rows name the same one
Outputs:
- correction: float32 [256, 64, 1024], P('lat', 'sec')
- weak_grad: float32 [64, 256], P('lat')
Inputs may be any that keep to these rules, and one draw needn't show every extreme that they name: `colors`: no two cells of one stencil (a cell and its six face neighbours) share a color. `weak_lines`: the entries of one device are distinct lines of its pencil block, numbered q = 16 * (x - 8 * s) + (y - 16 * l). `weak_owner`: among the rows of one device no owner is named more than 4 times; in some device some owner is named exactly 4 times.
All inputs are finite; a program needn't handle non-finite values. No bound on the sum of `yielded` on one device may be relied on, other than what follows from the above.
Results may differ from a plain program's by a relative error of at most 0.0003.
Values sent between devices are 32-bit elements; how exact they have to be, the bound alone decides.
No kernel may reach another device: no remote copies, remote signals or barrier semaphores. Data moves between devices by JAX's collectives and lax.ppermute only.
A program may use at most 64 MiB of HBM per device.

v0:
```python
import jax
import jax.numpy as jnp
from jax import lax
from jax.experimental import pallas as pl
from jax.experimental.pallas import tpu as pltpu
from jax.sharding import PartitionSpec as P

LANES = 128
ROWS = 8
FIELDS = 5
FINITE_STEP = 0.03125
YIELD_WEIGHT = 0.25
HIGHEST = lax.Precision.HIGHEST
VMEM = pl.BlockSpec(memory_space=pltpu.VMEM)
HBM = pl.BlockSpec(memory_space=pltpu.HBM)
MIB = 1024 * 1024


def viscosity(field, base, coef):
    return base / (1.0 + coef * field * field)


def rim_kernel(
    velocity_far,
    base_far,
    yielded_far,
    low_level,
    high_level,
    low_row,
    high_row,
    velocity,
    base,
    yielded,
    landed,
):
    arrays = ((velocity_far, velocity), (base_far, base), (yielded_far, yielded))
    copies = [pltpu.make_async_copy(far, near, landed.at[place]) for place, (far, near) in enumerate(arrays)]
    for copy in copies:
        copy.start()
    for copy in copies:
        copy.wait()
    levels = velocity.shape[0]
    rows = velocity.shape[1]
    for level in range(levels):
        v = velocity[level]
        eta = viscosity(v, base[level], yielded[level].astype(jnp.float32) * YIELD_WEIGHT)
        low_row[0, level, :] = v[0]
        low_row[1, level, :] = eta[0]
        high_row[0, level, :] = v[rows - 1]
        high_row[1, level, :] = eta[rows - 1]
        if level == 0:
            low_level[0] = v
            low_level[1] = eta
        if level == levels - 1:
            high_level[0] = v
            high_level[1] = eta


def turns():
    width = LANES // ROWS
    row = lax.broadcasted_iota(jnp.int32, (ROWS, LANES), 0)
    lane = lax.broadcasted_iota(jnp.int32, (ROWS, LANES), 1)
    return (lane // width - row) & (ROWS - 1), (lane + row * width) & (LANES - 1)


def to_lines(block, fetch):
    skewed = pltpu.roll(block, 0, 1, stride=LANES // ROWS, stride_axis=0)
    return jnp.take_along_axis(skewed, fetch[0], axis=0, mode="promise_in_bounds")


def to_cells(block, fetch):
    skewed = jnp.take_along_axis(block, fetch[0], axis=0, mode="promise_in_bounds")
    return jnp.take_along_axis(skewed, fetch[1], axis=1, mode="promise_in_bounds")


def tile_kernel(velocity, base, yielded, colors, forcing, below, above, left, right, out):
    levels, rows, width = velocity.shape
    fetch = turns()
    lane = lax.broadcasted_iota(jnp.int32, (rows, width), 1)
    row = lax.broadcasted_iota(jnp.int32, (rows, width), 0)
    fields = [below[0]] + [velocity[level] for level in range(levels)] + [above[0]]
    coefs = [yielded[level].astype(jnp.float32) * YIELD_WEIGHT for level in range(levels)]
    inverse = [
        1.0 / (1.0 + coefs[level] * fields[level + 1] * fields[level + 1]) for level in range(levels)
    ]
    etas = [below[1]] + [base[level] * inverse[level] for level in range(levels)] + [above[1]]

    def neighbours(centre, side, level):
        low_x = jnp.where(row == 0, left[side, level][None, :], pltpu.roll(centre, 1, 0))
        high_x = jnp.where(row == rows - 1, right[side, level][None, :], pltpu.roll(centre, rows - 1, 0))
        low_y = jnp.where(lane == 0, 0.0, pltpu.roll(centre, 1, 1))
        high_y = jnp.where(lane == width - 1, 0.0, pltpu.roll(centre, width - 1, 1))
        return low_x, high_x, low_y, high_y

    for level in range(levels):
        v = fields[level + 1]
        eta = etas[level + 1]
        b = base[level]
        coef = coefs[level]
        near_v = neighbours(v, 0, level) + (fields[level], fields[level + 2])
        near_eta = neighbours(eta, 1, level) + (etas[level], etas[level + 2])
        value_sum = near_v[0]
        eta_sum = near_eta[0]
        product_sum = near_v[0] * near_eta[0]
        for near_value, near_visc in zip(near_v[1:], near_eta[1:]):
            value_sum = value_sum + near_value
            eta_sum = eta_sum + near_visc
            product_sum = product_sum + near_value * near_visc
        spread = 6.0 * v - value_sum
        sensitivity = 0.5 * eta * spread
        residual = sensitivity + 0.5 * (v * eta_sum - product_sum) + b * v - forcing[level]
        step = FINITE_STEP * (colors[level] + 1).astype(jnp.float32)
        moved = v + step
        moved_inverse = 1.0 / (1.0 + coef * moved * moved)
        moved_eta = b * moved_inverse
        slope = -coef * (moved + v) * eta * moved_inverse
        diagonal = 0.5 * eta_sum + 3.0 * moved_eta + 0.5 * slope * spread + b
        onto_below = 0.5 * (slope * (fields[level] - v) - etas[level] - moved_eta)
        onto_above = 0.5 * (slope * (fields[level + 2] - v) - etas[level + 2] - moved_eta)
        for place, field in enumerate((residual, diagonal, onto_below, onto_above, sensitivity)):
            for block in range(width // LANES):
                lines = to_lines(field[:, block * LANES : (block + 1) * LANES], fetch)
                start = block * ROWS * FIELDS * levels + place * levels + level
                out[pl.ds(start, ROWS, stride=FIELDS * levels), :] = lines


def lines_kernel(line_ids, owner_ids, lines_of):
    entries = line_ids.shape[1]
    owner_count, line_count = lines_of.shape
    picks = (lax.broadcasted_iota(jnp.int32, (line_count, entries), 0) == line_ids[...]).astype(jnp.float32)
    owners = (lax.broadcasted_iota(jnp.int32, (owner_count, entries), 0) == owner_ids[...]).astype(jnp.float32)
    lines_of[...] = lax.dot_general(
        owners, picks, (((1,), (1,)), ((), ())), preferred_element_type=jnp.float32
    )


def pencil_kernel(levels, received, block_diag, block_below, block_above, lines_of, out, work):
    radial = work.shape[1]
    devices = radial // levels
    stride = FIELDS * levels
    for place in range(FIELDS):
        for level in range(levels):
            for group in range(devices // ROWS):
                work[place, pl.ds(group * ROWS * levels + level, ROWS, stride=levels), :] = received[
                    pl.ds(group * ROWS * stride + place * levels + level, ROWS, stride=stride), :
                ]
    residual = work[0]
    half = radial // 2

    def apply_blocks(field):
        head, tail = field[:half], field[half:]
        first = jnp.dot(block_diag[0], head, precision=HIGHEST, preferred_element_type=jnp.float32)
        first = first + jnp.dot(block_above[0], tail, precision=HIGHEST, preferred_element_type=jnp.float32)
        second = jnp.dot(block_diag[1], tail, precision=HIGHEST, preferred_element_type=jnp.float32)
        second = second + jnp.dot(block_below[1], head, precision=HIGHEST, preferred_element_type=jnp.float32)
        return jnp.concatenate([first, second], axis=0)

    initial = apply_blocks(residual)
    level_index = lax.broadcasted_iota(jnp.int32, (radial, LANES), 0)
    from_above = jnp.where(level_index == radial - 1, 0.0, pltpu.roll(work[2] * initial, radial - 1, 0))
    from_below = jnp.where(level_index == 0, 0.0, pltpu.roll(work[3] * initial, 1, 0))
    remainder = residual - (work[1] * initial + from_above + from_below)
    correction = initial + apply_blocks(remainder)
    gradient = correction * work[4]

    owned = lax.dot_general(
        lines_of[...],
        gradient,
        (((1,), (1,)), ((), ())),
        precision=HIGHEST,
        preferred_element_type=jnp.float32,
    )
    work[0] = correction
    parts = radial // LANES
    back = levels + parts
    for group in range(devices // ROWS):
        for level in range(levels):
            out[pl.ds(group * ROWS * back + level, ROWS, stride=back), :] = work[
                0, pl.ds(group * ROWS * levels + level, ROWS, stride=levels), :
            ]
        for part in range(parts):
            out[pl.ds(group * ROWS * back + levels + part, ROWS, stride=back), :] = owned[
                group * ROWS : (group + 1) * ROWS, part * LANES : (part + 1) * LANES
            ]


def owned_kernel(levels, received, owned):
    sectors, _, radial = owned.shape
    parts = radial // LANES
    back = levels + parts
    groups = received.shape[0] // (back * ROWS)
    for part in range(parts):
        total = received[pl.ds(levels + part, ROWS, stride=back), :]
        for group in range(1, groups):
            total = total + received[pl.ds(group * ROWS * back + levels + part, ROWS, stride=back), :]
        total = jnp.sum(total, axis=0, keepdims=True)
        for sector in range(sectors):
            owned[sector, :, part * LANES : (part + 1) * LANES] = total


def finish_kernel(received, correction):
    levels, rows, width = correction.shape
    groups = width // LANES
    back = received.shape[0] // (groups * ROWS)
    fetch = turns()
    for level in range(levels):
        for group in range(groups):
            lines = received[pl.ds(group * ROWS * back + level, ROWS, stride=back), :]
            correction[level, :, group * LANES : (group + 1) * LANES] = to_cells(lines, fetch)


def shifted(cells, axis, step):
    count = lax.axis_size(axis)
    return lax.ppermute(cells, axis, [(i, i + step) for i in range(count) if 0 <= i + step < count])


def swapped(rows, parts):
    devices = lax.axis_size("lat")
    sent = rows.reshape(devices, -1, parts, LANES)
    taken = lax.all_to_all(sent, "lat", split_axis=0, concat_axis=0, tiled=True)
    return taken.reshape(rows.shape)


def kernel_call(body, shapes, count, flops, name, scratch=(), place=VMEM, grant=32):
    total = sum(4 * size for size in flops[1:])
    return pl.pallas_call(
        body,
        out_shape=shapes,
        in_specs=[place] * count,
        out_specs=[VMEM] * len(shapes),
        scratch_shapes=scratch,
        compiler_params=pltpu.CompilerParams(vmem_limit_bytes=grant * MIB),
        cost_estimate=pl.CostEstimate(flops=flops[0], bytes_accessed=total, transcendentals=0),
        name=name,
    )


def f32(*shape):
    return jax.ShapeDtypeStruct(shape, jnp.float32)


def local(
    velocity,
    base_visc,
    yielded,
    colors,
    forcing,
    block_diag,
    block_below,
    block_above,
    weak_lines,
    weak_owner,
):
    levels, rows, width = velocity.shape
    devices = lax.axis_size("lat")
    sectors = lax.axis_size("sec")
    radial = levels * devices
    cells = levels * rows * width
    level_rim = f32(2, rows, width)
    row_rim = f32(2, levels, width)
    low_level, high_level, low_row, high_row = kernel_call(
        rim_kernel,
        [level_rim, level_rim, row_rim, row_rim],
        3,
        (4 * cells, 4 * cells),
        "rim",
        [
            pltpu.VMEM(velocity.shape, jnp.float32),
            pltpu.VMEM(velocity.shape, jnp.float32),
            pltpu.VMEM(velocity.shape, jnp.int32),
            pltpu.SemaphoreType.DMA((3,)),
        ],
        HBM,
        60,
    )(velocity, base_visc, yielded)
    left = shifted(high_row, "sec", 1)
    right = shifted(low_row, "sec", -1)
    below = shifted(high_level, "lat", 1)
    above = shifted(low_level, "lat", -1)
    (fields,) = kernel_call(
        tile_kernel,
        [f32(devices * FIELDS * levels, LANES)],
        9,
        (60 * cells, 12 * cells),
        "tile",
    )(velocity, base_visc, yielded, colors, forcing, below, above, left, right)
    fields = swapped(fields, levels)
    back = levels + radial // LANES

    picked = weak_lines.reshape(1, -1)
    line_width = LANES // rows
    place = (lax.axis_index("lat") + picked // line_width) % rows
    line_ids = place * line_width + picked % line_width

    (lines_of,) = kernel_call(
        lines_kernel, [f32(devices, LANES)], 2, (2 * devices * LANES * 64, devices * LANES), "lines"
    )(line_ids, weak_owner.reshape(1, -1))

    def pencil_body(*refs):
        pencil_kernel(levels, *refs)

    (improved,) = kernel_call(
        pencil_body,
        [f32(devices * back, LANES)],
        5,
        (24 * radial * radial * LANES, 12 * radial * LANES),
        "pencil",
        [pltpu.VMEM((FIELDS, radial, LANES), jnp.float32)],
    )(
        fields,
        block_diag,
        block_below,
        block_above,
        lines_of,
    )
    improved = swapped(improved, 2)

    def owned_body(*refs):
        owned_kernel(levels, *refs)

    (owned,) = kernel_call(
        owned_body, [f32(sectors, 1, radial)], 1, (devices * radial, devices * radial), "owned"
    )(improved)
    sums = lax.all_to_all(owned, "sec", split_axis=0, concat_axis=0, tiled=True)
    (correction,) = kernel_call(
        finish_kernel, [f32(levels, rows, width)], 1, (4 * cells, 3 * cells), "finish"
    )(improved)
    weak_grad = jnp.sum(sums, axis=0)
    return (correction, weak_grad)


def solution(mesh):
    return jax.shard_map(
        local,
        mesh=mesh,
        in_specs=(
            P("lat", "sec", None),
            P("lat", "sec", None),
            P("lat", "sec", None),
            P("lat", "sec", None),
            P("lat", "sec", None),
            P(),
            P(),
            P(),
            P("sec", "lat", None),
            P("sec", "lat", None, None),
        ),
        out_specs=(P("lat", "sec", None), P("lat", None)),
        check_vma=False,
    )
```

profile of v0, /device:TPU:1, one launch (start us, length us, event | category | flops | bytes accessed | tf_op | source)
XLA Modules:
  0.0 115.4 jit_solution(18104942463084647884)
XLA Ops:
  0.6 0.0 copy-start
  0.6 0.0 copy-start.1
  0.6 0.0 copy-start.2
  0.7 1.8 %rim.1 = (f32[2,8,1024]{2,1,0:T(8,128)}, f32[2,8,1024]{2,1,0:T(8,128)}, f32[2,4,1024]{2,1,0:T(4,128)}, f32[2,4,1024]{2,1,0:T(4,128)}) custom-call(f32[4,8,1024]{2,1,0:T(8,128)} %velocity.1, f32[4,8,1024]{2,1,0:T(8,128)} %base.1, s32[4,8,1024]{2,1,0:T(8,128)} %yielded.1), custom_call_target="tpu_custom_call" | custom-call | flops 131072 | bytes 524288 | tf_op jit(solution)/shard_map/rim/pallas_call | solution.py:261
  2.4 4.4 %collective-permute-start = (f32[2,8,1024]{2,1,0:T(8,128)}, f32[2,8,1024]{2,1,0:T(8,128)S(1)}, u32[]{:S(2)}, u32[]{:S(2)}) collective-permute-start(f32[2,8,1024]{2,1,0:T(8,128)} %get-tuple-element.6), channel_id=1, source_target_pairs={{0,8},{8,16},{16,24},{24,32},{32,40},{40,48},{48,56},{56,64},{64,7... | collective-permute-start | bytes 196616 | tf_op jit(solution)/shard_map/ppermute | solution.py:214
  6.8 1.3 %collective-permute-start.1 = (f32[2,8,1024]{2,1,0:T(8,128)}, f32[2,8,1024]{2,1,0:T(8,128)S(1)}, u32[]{:S(2)}, u32[]{:S(2)}) collective-permute-start(f32[2,8,1024]{2,1,0:T(8,128)} %get-tuple-element.7), channel_id=1, source_target_pairs={{8,0},{16,8},{24,16},{32,24},{40,32},{48,40},{56,48},{64,56},{72,6... | collective-permute-start | bytes 196616 | tf_op jit(solution)/shard_map/ppermute | solution.py:214
  8.1 4.0 %collective-permute-start.2 = (f32[2,4,1024]{2,1,0:T(4,128)}, f32[2,4,1024]{2,1,0:T(4,128)S(1)}, u32[]{:S(2)}, u32[]{:S(2)}) collective-permute-start(f32[2,4,1024]{2,1,0:T(4,128)} %get-tuple-element.8), channel_id=1, source_target_pairs={{0,1},{1,2},{2,3},{3,4},{4,5},{5,6},{6,7},{8,9},{9,10},{10,11},{11... | collective-permute-start | bytes 98312 | tf_op jit(solution)/shard_map/ppermute | solution.py:214
  12.2 3.0 %collective-permute-start.3 = (f32[2,4,1024]{2,1,0:T(4,128)}, f32[2,4,1024]{2,1,0:T(4,128)S(1)}, u32[]{:S(2)}, u32[]{:S(2)}) collective-permute-start(f32[2,4,1024]{2,1,0:T(4,128)} %get-tuple-element.9), channel_id=1, source_target_pairs={{1,0},{2,1},{3,2},{4,3},{5,4},{6,5},{7,6},{9,8},{10,9},{11,10},{12... | collective-permute-start | bytes 98312 | tf_op jit(solution)/shard_map/ppermute | solution.py:214
  15.1 0.0 collective-permute-done.2.left
  15.2 2.5 %collective-permute-done.3.right = f32[2,4,1024]{2,1,0:T(4,128)S(1)} collective-permute-done((f32[2,4,1024]{2,1,0:T(4,128)}, f32[2,4,1024]{2,1,0:T(4,128)S(1)}, u32[]{:S(2)}, u32[]{:S(2)}) %collective-permute-start.3) | collective-permute-done | bytes 32800 | tf_op jit(solution)/shard_map/ppermute | solution.py:214
  17.6 0.0 collective-permute-done.below
  17.6 0.0 collective-permute-done.1.above
  17.6 0.0 copy-done
  17.6 0.0 copy-done.1
  17.6 0.0 copy-done.2
  17.7 0.0 copy-start.3
  17.7 0.9 copy-done.3
  18.6 0.0 copy-start.4
  18.6 0.9 copy-done.4
  19.5 1.5 %tile.1 = f32[1280,128]{1,0:T(8,128)} custom-call(f32[4,8,1024]{2,1,0:T(8,128)S(1)} %copy-done, f32[4,8,1024]{2,1,0:T(8,128)S(1)} %copy-done.1, s32[4,8,1024]{2,1,0:T(8,128)S(1)} %copy-done.2, s32[4,8,1024]{2,1,0:T(8,128)S(1)} %copy-done.3, f32[4,8,1024]{2,1,0:T(8,128)S(1)} %copy-done.4, f32[2,8,1024]{2,1,0:T(8,128)S(1)} %collective-permute-done.below, ...), custom_call_target="tpu_custom_call" | custom-call | flops 1966080 | bytes 1572864 | tf_op jit(solution)/shard_map/tile/pallas_call | solution.py:280
  21.0 0.0 copy-start.5
  21.0 0.0 copy-start.6
  21.0 0.0 copy-start.7
  21.0 20.3 %all-to-all-start = ((f32[64,5,4,128]{3,2,1,0:T(4,128)}), f32[64,5,4,128]{3,2,1,0:T(4,128)S(1)}, u32[]{:S(2)}, u32[]{:S(2)}) async-start(f32[64,5,4,128]{3,2,1,0:T(4,128)} %bitcast), calls=%async_computation | async-start | bytes 1310720 | tf_op jit(solution)/shard_map/all_to_all | solution.py:220
  41.3 0.0 copy-start.9
  41.3 0.6 copy-done.9
  42.0 0.0 copy-start.8
  42.0 0.6 copy-done.8
  42.7 0.1 lines.1.refs_4_
  42.8 34.6 %all-to-all-done = f32[64,5,4,128]{3,2,1,0:T(4,128)S(1)} async-done(((f32[64,5,4,128]{3,2,1,0:T(4,128)}), f32[64,5,4,128]{3,2,1,0:T(4,128)S(1)}, u32[]{:S(2)}, u32[]{:S(2)}) %all-to-all-start) | async-done | bytes 655392 | tf_op jit(solution)/shard_map/all_to_all | solution.py:220
  77.4 0.0 copy-done.5
  77.4 0.0 copy-done.6
  77.4 0.0 copy-done.7
  77.4 1.0 pencil.1
  78.4 23.1 %all_to_all.15 = f32[64,3,2,128]{3,2,1,0:T(2,128)S(1)} all-to-all(f32[64,3,2,128]{3,2,1,0:T(2,128)S(1)} %bitcast.22), channel_id=1, replica_groups=mesh['lat'=64,'sec'=8] {'lat'}, dimensions={0} | all-to-all | bytes 393216 | tf_op jit(solution)/shard_map/all_to_all | solution.py:220
  101.5 0.6 owned.1
  102.1 8.1 %all-to-all-start.2 = ((f32[8,1,256]{2,1,0:T(1,128)}), f32[8,1,256]{2,1,0:T(1,128)S(1)}, u32[]{:S(2)}, u32[]{:S(2)}) async-start(f32[8,1,256]{2,1,0:T(1,128)} %owned.1), calls=%async_computation.2 | async-start | bytes 16384 | tf_op jit(solution)/shard_map/all_to_all | solution.py:324
  110.2 0.8 finish.1
  110.9 3.8 %all-to-all-done.2 = f32[8,1,256]{2,1,0:T(1,128)S(1)} async-done(((f32[8,1,256]{2,1,0:T(1,128)}), f32[8,1,256]{2,1,0:T(1,128)S(1)}, u32[]{:S(2)}, u32[]{:S(2)}) %all-to-all-start.2) | async-done | bytes 8224 | tf_op jit(solution)/shard_map/all_to_all | solution.py:324
  114.8 0.6 reduce_sum.11
  (1 shorter events, 0.0 us)
Async XLA Ops:
  0.6 17.0 %copy-start = (f32[4,8,1024]{2,1,0:T(8,128)S(1)}, f32[4,8,1024]{2,1,0:T(8,128)}, u32[]{:S(2)}) copy-start(f32[4,8,1024]{2,1,0:T(8,128)} %velocity.1) | copy-start | bytes 393220
  0.6 17.0 %copy-start.1 = (f32[4,8,1024]{2,1,0:T(8,128)S(1)}, f32[4,8,1024]{2,1,0:T(8,128)}, u32[]{:S(2)}) copy-start(f32[4,8,1024]{2,1,0:T(8,128)} %base.1) | copy-start | bytes 393220
  0.6 17.0 %copy-start.2 = (s32[4,8,1024]{2,1,0:T(8,128)S(1)}, s32[4,8,1024]{2,1,0:T(8,128)}, u32[]{:S(2)}) copy-start(s32[4,8,1024]{2,1,0:T(8,128)} %yielded.1) | copy-start | bytes 393220
  2.4 15.2 %collective-permute-start = (f32[2,8,1024]{2,1,0:T(8,128)}, f32[2,8,1024]{2,1,0:T(8,128)S(1)}, u32[]{:S(2)}, u32[]{:S(2)}) collective-permute-start(f32[2,8,1024]{2,1,0:T(8,128)} %get-tuple-element.6), channel_id=1, source_target_pairs={{0,8},{8,16},{16,24},{24,32},{32,40},{40,48},{48,56},{56,64},{64,7... | collective-permute-start | bytes 196616 | tf_op jit(solution)/shard_map/ppermute | solution.py:214
  6.8 10.8 %collective-permute-start.1 = (f32[2,8,1024]{2,1,0:T(8,128)}, f32[2,8,1024]{2,1,0:T(8,128)S(1)}, u32[]{:S(2)}, u32[]{:S(2)}) collective-permute-start(f32[2,8,1024]{2,1,0:T(8,128)} %get-tuple-element.7), channel_id=1, source_target_pairs={{8,0},{16,8},{24,16},{32,24},{40,32},{48,40},{56,48},{64,56},{72,6... | collective-permute-start | bytes 196616 | tf_op jit(solution)/shard_map/ppermute | solution.py:214
  8.1 7.0 %collective-permute-start.2 = (f32[2,4,1024]{2,1,0:T(4,128)}, f32[2,4,1024]{2,1,0:T(4,128)S(1)}, u32[]{:S(2)}, u32[]{:S(2)}) collective-permute-start(f32[2,4,1024]{2,1,0:T(4,128)} %get-tuple-element.8), channel_id=1, source_target_pairs={{0,1},{1,2},{2,3},{3,4},{4,5},{5,6},{6,7},{8,9},{9,10},{10,11},{11... | collective-permute-start | bytes 98312 | tf_op jit(solution)/shard_map/ppermute | solution.py:214
  12.2 5.4 %collective-permute-start.3 = (f32[2,4,1024]{2,1,0:T(4,128)}, f32[2,4,1024]{2,1,0:T(4,128)S(1)}, u32[]{:S(2)}, u32[]{:S(2)}) collective-permute-start(f32[2,4,1024]{2,1,0:T(4,128)} %get-tuple-element.9), channel_id=1, source_target_pairs={{1,0},{2,1},{3,2},{4,3},{5,4},{6,5},{7,6},{9,8},{10,9},{11,10},{12... | collective-permute-start | bytes 98312 | tf_op jit(solution)/shard_map/ppermute | solution.py:214
  17.7 0.9 copy-start.3
  18.6 0.9 copy-start.4
  21.0 56.4 %copy-start.5 = (f32[2,128,128]{2,1,0:T(8,128)S(1)}, f32[2,128,128]{2,1,0:T(8,128)}, u32[]{:S(2)}) copy-start(f32[2,128,128]{2,1,0:T(8,128)} %refs_1_.1) | copy-start | bytes 393220
  21.0 56.4 %copy-start.6 = (f32[2,128,128]{2,1,0:T(8,128)S(1)}, f32[2,128,128]{2,1,0:T(8,128)}, u32[]{:S(2)}) copy-start(f32[2,128,128]{2,1,0:T(8,128)} %refs_2_.1) | copy-start | bytes 393220
  21.0 56.4 %copy-start.7 = (f32[2,128,128]{2,1,0:T(8,128)S(1)}, f32[2,128,128]{2,1,0:T(8,128)}, u32[]{:S(2)}) copy-start(f32[2,128,128]{2,1,0:T(8,128)} %refs_3_.1) | copy-start | bytes 393220
  21.0 56.4 %all-to-all-start = ((f32[64,5,4,128]{3,2,1,0:T(4,128)}), f32[64,5,4,128]{3,2,1,0:T(4,128)S(1)}, u32[]{:S(2)}, u32[]{:S(2)}) async-start(f32[64,5,4,128]{3,2,1,0:T(4,128)} %bitcast), calls=%async_computation | async-start | bytes 1310720 | tf_op jit(solution)/shard_map/all_to_all | solution.py:220
  41.3 0.7 copy-start.9
  42.0 0.7 copy-start.8
  102.1 12.7 %all-to-all-start.2 = ((f32[8,1,256]{2,1,0:T(1,128)}), f32[8,1,256]{2,1,0:T(1,128)S(1)}, u32[]{:S(2)}, u32[]{:S(2)}) async-start(f32[8,1,256]{2,1,0:T(1,128)} %owned.1), calls=%async_computation.2 | async-start | bytes 16384 | tf_op jit(solution)/shard_map/all_to_all | solution.py:324
where the time goes:
time: 116 us; the launch traced here: 115 us
  starting transfers between devices  41.1 us (35%)
  waiting for transfers between devices  40.9 us (35%)
  blocking collectives  23.1 us (20%)
  Pallas kernels  5.82 us (5%)
  local copies, waits for them, and re-layouts  3.13 us (3%)
    all_to_all x1, waiting for transfers between devices, swapped(): taken = lax.all_to_all(sent, 'lat', split_axis=0, concat_axis=0, tiled=True)  34.6 us
    all_to_all x1, blocking collectives, swapped(): taken = lax.all_to_all(sent, 'lat', split_axis=0, concat_axis=0, tiled=True)  23.1 us
    all_to_all x1, starting transfers between devices, swapped(): taken = lax.all_to_all(sent, 'lat', split_axis=0, concat_axis=0, tiled=True)  20.3 us
    ppermute x4, starting transfers between devices, shifted(): lax.ppermute(cells, axis, [(i, i + step) for i in range(count) if 0 <= i...  12.7 us
    all_to_all x1, starting transfers between devices, local(): sums = lax.all_to_all(owned, 'sec', split_axis=0, concat_axis=0, tiled=True)  8.05 us
    all_to_all x1, waiting for transfers between devices, local(): sums = lax.all_to_all(owned, 'sec', split_axis=0, concat_axis=0, tiled=True)  3.85 us
    unnamed x20, local copies, waits for them, and re-layouts  3.13 us
    ppermute x4, waiting for transfers between devices, shifted(): lax.ppermute(cells, axis, [(i, i + step) for i in range(count) if 0 <= i...  2.48 us
  transfers between devices with their start and end apart: 6, of which 3 were waited for; matrix products, arithmetic and copies ran while one was open for 0% of the time, Pallas kernels for 1%

commit v1 on v0

v1 whole, which is shorter than its diff:
```python
import jax
import jax.numpy as jnp
from jax import lax
from jax.experimental import pallas as pl
from jax.experimental.pallas import tpu as pltpu
from jax.sharding import PartitionSpec as P

LANES = 128
ROWS = 8
WIDTH = LANES // ROWS
FIELDS = 5
SENT = FIELDS + 1
FINITE_STEP = 0.03125
YIELD_WEIGHT = 0.25
HIGHEST = lax.Precision.HIGHEST
VMEM = pl.BlockSpec(memory_space=pltpu.VMEM)
HBM = pl.BlockSpec(memory_space=pltpu.HBM)
SMEM = pl.BlockSpec(memory_space=pltpu.SMEM)
MIB = 1024 * 1024


def places():
    row = lax.broadcasted_iota(jnp.int32, (ROWS, LANES), 0)
    lane = lax.broadcasted_iota(jnp.int32, (ROWS, LANES), 1)
    return row, lane // WIDTH, lane % WIDTH


def along_lane(block, row_of):
    return jnp.take_along_axis(block, row_of, axis=0, mode="promise_in_bounds")


def along_row(block, lane_of):
    return jnp.take_along_axis(block, lane_of, axis=1, mode="promise_in_bounds")


def to_lines(block, row_of):
    return along_lane(pltpu.roll(block, 0, 1, stride=WIDTH, stride_axis=0), row_of)


def cells_kernel(
    velocity_far,
    base_far,
    yielded_far,
    colors_far,
    forcing_far,
    cells,
    low_row,
    high_row,
    velocity,
    base,
    yielded,
    colors,
    landed,
):
    forcing = cells.at[FIELDS - 1]
    arrays = (
        (velocity_far, velocity),
        (base_far, base),
        (yielded_far, yielded),
        (colors_far, colors),
        (forcing_far, forcing),
    )
    copies = [pltpu.make_async_copy(far, near, landed.at[place]) for place, (far, near) in enumerate(arrays)]
    for copy in copies:
        copy.start()
    for copy in copies:
        copy.wait()
    levels, rows, _ = velocity.shape
    for level in range(levels):
        v = velocity[level]
        b = base[level]
        coef = yielded[level].astype(jnp.float32) * YIELD_WEIGHT
        eta = b / (1.0 + coef * v * v)
        cells[0, level] = v
        cells[1, level] = b
        cells[2, level] = coef
        cells[3, level] = FINITE_STEP * (colors[level] + 1).astype(jnp.float32)
        cells[FIELDS, level] = eta
        low_row[0, level, :] = v[0]
        low_row[1, level, :] = eta[0]
        high_row[0, level, :] = v[rows - 1]
        high_row[1, level, :] = eta[rows - 1]


def tile_kernel(cells, lines):
    _, levels, _, width = cells.shape
    row, group, _ = places()
    row_of = (group - row) & (ROWS - 1)
    for field in range(FIELDS):
        for level in range(levels):
            for block in range(width // LANES):
                lines[field, level, block] = to_lines(
                    cells[field, level, :, block * LANES : (block + 1) * LANES], row_of
                )


def rim_kernel(lines, cells, left, right, out):
    _, levels, _, width = cells.shape
    stride = SENT * levels
    blocks = width // LANES
    row, group, place = places()
    row_of = (group - row) & (ROWS - 1)
    lane = group * WIDTH + place
    low_lane = (((group - 1) & (ROWS - 1)) * WIDTH - 1) & (LANES - 1)
    high_lane = (((group - 2) & (ROWS - 1)) * WIDTH + WIDTH) & (LANES - 1)
    x_of = place & (ROWS - 1)
    for level in range(levels):
        for block in range(blocks):
            start = block * ROWS * stride + level
            for field in range(FIELDS):
                out[pl.ds(start + field * levels, ROWS, stride=stride), :] = lines[field, level, block]
            span = slice(block * LANES, (block + 1) * LANES)
            ends = jnp.where(
                row == 0,
                left[0, level, span][None, :],
                jnp.where(
                    row == 7,
                    right[0, level, span][None, :],
                    jnp.where(row == 4, left[1, level, span][None, :], right[1, level, span][None, :]),
                ),
            )
            lows = []
            highs = []
            for kind in (0, FIELDS):
                here = cells[kind, level, :, span]
                low = here
                high = here
                if block > 0:
                    before = cells[kind, level, :, slice((block - 1) * LANES, block * LANES)]
                    low = jnp.where(lane == LANES - 1, before, here)
                else:
                    low = jnp.where(lane == LANES - 1, 0.0, here)
                if block < blocks - 1:
                    after = cells[kind, level, :, slice((block + 1) * LANES, (block + 2) * LANES)]
                    high = jnp.where(lane == 0, after, here)
                else:
                    high = jnp.where(lane == 0, 0.0, here)
                lows.append(along_row(low, low_lane))
                highs.append(along_row(high, high_lane))
            low = along_lane(jnp.where(place < ROWS, lows[0], lows[1]), x_of)
            high = along_lane(jnp.where(place < ROWS, highs[0], highs[1]), x_of)
            slot = row_of
            whole = jnp.where(slot == 1, low, jnp.where(slot == 2, high, to_lines(ends, row_of)))
            out[pl.ds(start + FIELDS * levels, ROWS, stride=stride), :] = whole


def lines_kernel(line_ids, owner_ids, lines_of):
    entries = line_ids.shape[1]
    owner_count, line_count = lines_of.shape
    picks = (lax.broadcasted_iota(jnp.int32, (line_count, entries), 0) == line_ids[...]).astype(jnp.float32)
    owners = (lax.broadcasted_iota(jnp.int32, (owner_count, entries), 0) == owner_ids[...]).astype(jnp.float32)
    lines_of[...] = lax.dot_general(
        owners, picks, (((1,), (1,)), ((), ())), preferred_element_type=jnp.float32
    )


def pencil_kernel(
    levels,
    received,
    turn,
    block_diag,
    block_below,
    block_above,
    lines_of,
    out,
    work,
    velocity,
    viscosity,
):
    radial = work.shape[1]
    devices = radial // levels
    stride = SENT * levels
    velocity[pl.ds(0, ROWS), :] = jnp.zeros((ROWS, LANES), jnp.float32)
    velocity[pl.ds(radial + ROWS, ROWS), :] = jnp.zeros((ROWS, LANES), jnp.float32)
    viscosity[pl.ds(0, ROWS), :] = jnp.zeros((ROWS, LANES), jnp.float32)
    viscosity[pl.ds(radial + ROWS, ROWS), :] = jnp.zeros((ROWS, LANES), jnp.float32)
    for place in range(SENT):
        for level in range(levels):
            for group in range(devices // ROWS):
                rows = received[pl.ds(group * ROWS * stride + place * levels + level, ROWS, stride=stride), :]
                target = group * ROWS * levels + level
                if place == 0:
                    velocity[pl.ds(ROWS + target, ROWS, stride=levels), :] = rows
                else:
                    work[place, pl.ds(target, ROWS, stride=levels), :] = rows
    for start in range(0, radial, ROWS):
        v = velocity[pl.ds(ROWS + start, ROWS), :]
        viscosity[pl.ds(ROWS + start, ROWS), :] = work[1, pl.ds(start, ROWS), :] / (
            1.0 + work[2, pl.ds(start, ROWS), :] * v * v
        )

    _, group, place = places()
    shift = turn[0, 0]
    x = (group - shift) & (ROWS - 1)
    first_x, last_x = x == 0, x == ROWS - 1
    first_y, last_y = place == 0, place == WIDTH - 1
    side = jnp.where(first_y, (shift + 1) & (ROWS - 1), (shift + 2) & (ROWS - 1))
    v_lane = side * WIDTH + x
    eta_lane = v_lane + ROWS

    def lateral(block, x_rim, y_rim):
        return (
            jnp.where(first_x, x_rim, pltpu.roll(block, WIDTH, 1)),
            jnp.where(last_x, x_rim, pltpu.roll(block, LANES - WIDTH, 1)),
            jnp.where(first_y, y_rim, pltpu.roll(block, 1, 1)),
            jnp.where(last_y, y_rim, pltpu.roll(block, LANES - 1, 1)),
        )

    for start in range(0, radial, ROWS):
        here = pl.ds(start, ROWS)
        v = velocity[pl.ds(ROWS + start, ROWS), :]
        v_low = velocity[pl.ds(ROWS + start - 1, ROWS), :]
        v_high = velocity[pl.ds(ROWS + start + 1, ROWS), :]
        eta = viscosity[pl.ds(ROWS + start, ROWS), :]
        eta_low = viscosity[pl.ds(ROWS + start - 1, ROWS), :]
        eta_high = viscosity[pl.ds(ROWS + start + 1, ROWS), :]
        b, coef, step, forcing = (work[field, here, :] for field in range(1, FIELDS))
        rim = work[FIELDS, here, :]
        near_v = lateral(v, rim, along_row(rim, v_lane)) + (v_low, v_high)
        near_eta = lateral(eta, pltpu.roll(rim, LANES // 2, 1), along_row(rim, eta_lane)) + (eta_low, eta_high)
        value_sum = near_v[0]
        eta_sum = near_eta[0]
        product_sum = near_v[0] * near_eta[0]
        for near_value, near_visc in zip(near_v[1:], near_eta[1:]):
            value_sum = value_sum + near_value
            eta_sum = eta_sum + near_visc
            product_sum = product_sum + near_value * near_visc
        spread = 6.0 * v - value_sum
        sensitivity = 0.5 * eta * spread
        moved = v + step
        moved_inverse = 1.0 / (1.0 + coef * moved * moved)
        moved_eta = b * moved_inverse
        slope = -coef * (moved + v) * eta * moved_inverse
        work[0, here, :] = sensitivity + 0.5 * (v * eta_sum - product_sum) + b * v - forcing
        work[1, here, :] = 0.5 * eta_sum + 3.0 * moved_eta + 0.5 * slope * spread + b
        work[2, here, :] = 0.5 * (slope * (v_low - v) - eta_low - moved_eta)
        work[3, here, :] = 0.5 * (slope * (v_high - v) - eta_high - moved_eta)
        work[4, here, :] = sensitivity

    residual = work[0]
    half = radial // 2

    def apply_blocks(field):
        head, tail = field[:half], field[half:]
        first = jnp.dot(block_diag[0], head, precision=HIGHEST, preferred_element_type=jnp.float32)
        first = first + jnp.dot(block_above[0], tail, precision=HIGHEST, preferred_element_type=jnp.float32)
        second = jnp.dot(block_diag[1], tail, precision=HIGHEST, preferred_element_type=jnp.float32)
        second = second + jnp.dot(block_below[1], head, precision=HIGHEST, preferred_element_type=jnp.float32)
        return jnp.concatenate([first, second], axis=0)

    initial = apply_blocks(residual)
    level_index = lax.broadcasted_iota(jnp.int32, (radial, LANES), 0)
    from_above = jnp.where(level_index == radial - 1, 0.0, pltpu.roll(work[2] * initial, radial - 1, 0))
    from_below = jnp.where(level_index == 0, 0.0, pltpu.roll(work[3] * initial, 1, 0))
    remainder = residual - (work[1] * initial + from_above + from_below)
    correction = initial + apply_blocks(remainder)
    gradient = correction * work[4]
    owned = lax.dot_general(
        lines_of[...],
        gradient,
        (((1,), (1,)), ((), ())),
        precision=HIGHEST,
        preferred_element_type=jnp.float32,
    )
    work[0] = correction
    parts = radial // LANES
    back = levels + parts
    for block in range(devices // ROWS):
        for level in range(levels):
            out[pl.ds(block * ROWS * back + level, ROWS, stride=back), :] = work[
                0, pl.ds(block * ROWS * levels + level, ROWS, stride=levels), :
            ]
        for part in range(parts):
            out[pl.ds(block * ROWS * back + levels + part, ROWS, stride=back), :] = owned[
                block * ROWS : (block + 1) * ROWS, part * LANES : (part + 1) * LANES
            ]


def owned_kernel(levels, received, owned):
    sectors, _, radial = owned.shape
    parts = radial // LANES
    back = levels + parts
    blocks = received.shape[0] // (back * ROWS)
    for part in range(parts):
        total = received[pl.ds(levels + part, ROWS, stride=back), :]
        for block in range(1, blocks):
            total = total + received[pl.ds(block * ROWS * back + levels + part, ROWS, stride=back), :]
        total = jnp.sum(total, axis=0, keepdims=True)
        for sector in range(sectors):
            owned[sector, :, part * LANES : (part + 1) * LANES] = total


def finish_kernel(received, correction):
    levels, rows, width = correction.shape
    blocks = width // LANES
    back = received.shape[0] // (blocks * ROWS)
    row, group, place = places()
    row_of = (group - row) & (ROWS - 1)
    lane_of = ((group + row) & (ROWS - 1)) * WIDTH + place
    for level in range(levels):
        for block in range(blocks):
            lines = received[pl.ds(block * ROWS * back + level, ROWS, stride=back), :]
            correction[level, :, block * LANES : (block + 1) * LANES] = along_row(
                along_lane(lines, row_of), lane_of
            )


def shifted(cells, axis, step):
    count = lax.axis_size(axis)
    return lax.ppermute(cells, axis, [(i, i + step) for i in range(count) if 0 <= i + step < count])


def swapped(rows, parts):
    devices = lax.axis_size("lat")
    sent = rows.reshape(devices, -1, parts, LANES)
    taken = lax.all_to_all(sent, "lat", split_axis=0, concat_axis=0, tiled=True)
    return taken.reshape(rows.shape)


def kernel_call(body, shapes, specs, work, name, scratch=()):
    return pl.pallas_call(
        body,
        out_shape=shapes,
        in_specs=specs,
        out_specs=[VMEM] * len(shapes),
        scratch_shapes=scratch,
        compiler_params=pltpu.CompilerParams(vmem_limit_bytes=32 * MIB),
        cost_estimate=pl.CostEstimate(flops=work[0], bytes_accessed=4 * work[1], transcendentals=0),
        name=name,
    )


def f32(*shape):
    return jax.ShapeDtypeStruct(shape, jnp.float32)


def local(
    velocity,
    base_visc,
    yielded,
    colors,
    forcing,
    block_diag,
    block_below,
    block_above,
    weak_lines,
    weak_owner,
):
    levels, rows, width = velocity.shape
    devices = lax.axis_size("lat")
    sectors = lax.axis_size("sec")
    radial = levels * devices
    cell_count = levels * rows * width
    row_shape = f32(2, levels, width)
    tile = (levels, rows, width)
    placed = f32(FIELDS, levels, width // LANES, ROWS, LANES)
    far = [
        pltpu.with_memory_space_constraint(array, pltpu.HBM)
        for array in (velocity, base_visc, yielded, colors, forcing)
    ]
    cells, low_row, high_row = kernel_call(
        cells_kernel,
        [f32(SENT, *tile), row_shape, row_shape],
        [HBM] * FIELDS,
        (20 * cell_count, 12 * cell_count),
        "cells",
        [pltpu.VMEM(tile, array.dtype) for array in far[:-1]] + [pltpu.SemaphoreType.DMA((FIELDS,))],
    )(*far)
    left = shifted(high_row, "sec", 1)
    right = shifted(low_row, "sec", -1)
    (lines,) = kernel_call(tile_kernel, [placed], [VMEM], (20 * cell_count, 10 * cell_count), "tile")(cells)
    (lines,) = kernel_call(
        rim_kernel,
        [f32(devices * SENT * levels, LANES)],
        [VMEM] * 4,
        (20 * cell_count, 12 * cell_count),
        "rims",
    )(lines, cells, left, right)
    lines = swapped(lines, levels)

    picked = weak_lines.reshape(1, -1)
    turn = lax.axis_index("lat") & (rows - 1)
    place = (turn + picked // WIDTH) & (rows - 1)
    line_ids = place * WIDTH + picked % WIDTH
    (lines_of,) = kernel_call(
        lines_kernel,
        [f32(devices, LANES)],
        [VMEM] * 2,
        (2 * devices * LANES * 64, devices * LANES),
        "lines",
    )(line_ids, weak_owner.reshape(1, -1))
    back = levels + radial // LANES

    def pencil_body(*refs):
        pencil_kernel(levels, *refs)

    (improved,) = kernel_call(
        pencil_body,
        [f32(devices * back, LANES)],
        [VMEM, SMEM, VMEM, VMEM, VMEM, VMEM],
        (24 * radial * radial * LANES, 12 * radial * LANES),
        "pencil",
        [
            pltpu.VMEM((SENT, radial, LANES), jnp.float32),
            pltpu.VMEM((radial + 2 * ROWS, LANES), jnp.float32),
            pltpu.VMEM((radial + 2 * ROWS, LANES), jnp.float32),
        ],
    )(lines, turn.astype(jnp.int32).reshape(1, 1), block_diag, block_below, block_above, lines_of)
    improved = swapped(improved, 2)

    def owned_body(*refs):
        owned_kernel(levels, *refs)

    (owned,) = kernel_call(
        owned_body, [f32(sectors, 1, radial)], [VMEM], (devices * radial, devices * radial), "owned"
    )(improved)
    sums = lax.all_to_all(owned, "sec", split_axis=0, concat_axis=0, tiled=True)
    (correction,) = kernel_call(
        finish_kernel, [f32(*tile)], [VMEM], (4 * cell_count, 3 * cell_count), "finish"
    )(improved)
    weak_grad = jnp.sum(sums, axis=0)
    return (correction, weak_grad)


def solution(mesh):
    return jax.shard_map(
        local,
        mesh=mesh,
        in_specs=(
            P("lat", "sec", None),
            P("lat", "sec", None),
            P("lat", "sec", None),
            P("lat", "sec", None),
            P("lat", "sec", None),
            P(),
            P(),
            P(),
            P("sec", "lat", None),
            P("sec", "lat", None, None),
        ),
        out_specs=(P("lat", "sec", None), P("lat", None)),
        check_vma=False,
    )
```

time: 116 us -> 112 us (0.966)
  starting transfers between devices: 41.1 us -> 35.3 us
  waiting for transfers between devices: 40.9 us -> 44.4 us
  local copies, waits for them, and re-layouts: 3.13 us -> 1.31 us
    all_to_all x1, waiting for transfers between devices: 34.6 us -> 40 us  [swapped(): taken = lax.all_to_all(sent, 'lat', split_axis=0, concat_axis=0, tiled=True)]
    all_to_all x1, starting transfers between devices: 20.3 us -> 17.3 us  [swapped(): taken = lax.all_to_all(sent, 'lat', split_axis=0, concat_axis=0, tiled=True)]
    ppermute x4 -> x2, starting transfers between devices: 12.7 us -> 10.1 us  [shifted(): lax.ppermute(cells, axis, [(i, i + step) for i in range(count) if 0 <= i...]
    ppermute x4 -> x2, waiting for transfers between devices: 2.48 us -> 0.59 us  [shifted(): lax.ppermute(cells, axis, [(i, i + step) for i in range(count) if 0 <= i...]
    unnamed x20 -> x10, local copies, waits for them, and re-layouts: 3.13 us -> 1.31 us
    pallas_call x6 -> x7, Pallas kernels: 5.82 us -> 5.86 us  [the longest x1 1.57 us: local(): kernel_call(pencil_body, [f32(devices * back, LANES)], [VMEM, SMEM, VMEM,...]
  transfers between devices with their start and end apart: 6 -> 4, of which waited for: 3 -> 3; matrix products, arithmetic and copies ran while one was open for 0% -> 0% of each run, Pallas kernels for 1% -> 1%
where the time goes in v1:
time: 112 us
  waiting for transfers between devices  44.4 us (40%)
  starting transfers between devices  35.3 us (32%)
  blocking collectives  23.3 us (21%)
  Pallas kernels  5.86 us (5%)
  local copies, waits for them, and re-layouts  1.31 us (1%)
    all_to_all x1, waiting for transfers between devices, swapped(): taken = lax.all_to_all(sent, 'lat', split_axis=0, concat_axis=0, tiled=True)  40 us
    all_to_all x1, blocking collectives, swapped(): taken = lax.all_to_all(sent, 'lat', split_axis=0, concat_axis=0, tiled=True)  23.3 us
    all_to_all x1, starting transfers between devices, swapped(): taken = lax.all_to_all(sent, 'lat', split_axis=0, concat_axis=0, tiled=True)  17.3 us
    ppermute x2, starting transfers between devices, shifted(): lax.ppermute(cells, axis, [(i, i + step) for i in range(count) if 0 <= i...  10.1 us
    all_to_all x1, starting transfers between devices, local(): sums = lax.all_to_all(owned, 'sec', split_axis=0, concat_axis=0, tiled=True)  7.92 us
    all_to_all x1, waiting for transfers between devices, local(): sums = lax.all_to_all(owned, 'sec', split_axis=0, concat_axis=0, tiled=True)  3.85 us
  transfers between devices with their start and end apart: 4, of which 3 were waited for; matrix products, arithmetic and copies ran while one was open for 0% of the time, Pallas kernels for 1%

profile of v1, /device:TPU:1, one launch (start us, length us, event | category | flops | bytes accessed | tf_op | source)
XLA Modules:
  0.0 111.5 jit_solution(12081575518951846025)
XLA Ops:
  0.6 1.3 %cells.1 = (f32[6,4,8,1024]{3,2,1,0:T(8,128)S(1)}, f32[2,4,1024]{2,1,0:T(4,128)S(1)}, f32[2,4,1024]{2,1,0:T(4,128)S(1)}) custom-call(f32[4,8,1024]{2,1,0:T(8,128)} %velocity_far.1, f32[4,8,1024]{2,1,0:T(8,128)} %base_far.1, s32[4,8,1024]{2,1,0:T(8,128)} %yielded_far.1, s32[4,8,1024]{2,1,0:T(8,128)} %colors_far.1, f32[4,8,1024]{2,1,0:T(8,128)} %forcing_far.1), custom_call_target="tpu_custom_call" | custom-call | flops 655360 | bytes 1572864 | tf_op jit(solution)/shard_map/cells/pallas_call | solution.py:361
  1.9 4.6 %collective-permute-start = (f32[2,4,1024]{2,1,0:T(4,128)S(1)}, f32[2,4,1024]{2,1,0:T(4,128)S(1)}, u32[]{:S(2)}, u32[]{:S(2)}) collective-permute-start(f32[2,4,1024]{2,1,0:T(4,128)S(1)} %get-tuple-element.6), channel_id=1, source_target_pairs={{0,1},{1,2},{2,3},{3,4},{4,5},{5,6},{6,7},{8,9},{9,10},{10,11},{11... | collective-permute-start | bytes 98312 | tf_op jit(solution)/shard_map/ppermute | solution.py:310
  6.5 5.5 %collective-permute-start.1 = (f32[2,4,1024]{2,1,0:T(4,128)S(1)}, f32[2,4,1024]{2,1,0:T(4,128)S(1)}, u32[]{:S(2)}, u32[]{:S(2)}) collective-permute-start(f32[2,4,1024]{2,1,0:T(4,128)S(1)} %get-tuple-element.7), channel_id=1, source_target_pairs={{1,0},{2,1},{3,2},{4,3},{5,4},{6,5},{7,6},{9,8},{10,9},{11,10},{12... | collective-permute-start | bytes 98312 | tf_op jit(solution)/shard_map/ppermute | solution.py:310
  12.0 0.2 tile.1.lines
  12.3 0.0 collective-permute-done.left
  12.3 0.6 collective-permute-done.1.right
  12.9 1.3 %rims.1 = f32[1536,128]{1,0:T(8,128)} custom-call(f32[5,4,8,8,128]{4,3,2,1,0:T(8,128)S(1)} %tile.1.lines, f32[6,4,8,1024]{3,2,1,0:T(8,128)S(1)} %get-tuple-element.5.cells, f32[2,4,1024]{2,1,0:T(4,128)S(1)} %collective-permute-done.left, f32[2,4,1024]{2,1,0:T(4,128)S(1)} %collective-permute-done.1.right), custom_call_target="tpu_custom_call" | custom-call | flops 655360 | bytes 1572864 | tf_op jit(solution)/shard_map/rims/pallas_call | solution.py:372
  14.1 0.0 copy-start
  14.1 0.0 copy-start.1
  14.1 0.0 copy-start.2
  14.1 17.3 %all-to-all-start = ((f32[64,6,4,128]{3,2,1,0:T(4,128)}), f32[64,6,4,128]{3,2,1,0:T(4,128)S(1)}, u32[]{:S(2)}, u32[]{:S(2)}) async-start(f32[64,6,4,128]{3,2,1,0:T(4,128)} %bitcast), calls=%async_computation | async-start | bytes 1572864 | tf_op jit(solution)/shard_map/all_to_all | solution.py:316
  31.4 0.0 copy-start.4
  31.5 0.6 copy-done.4
  32.1 0.0 copy-start.3
  32.1 0.6 copy-done.3
  32.8 0.1 lines.1.refs_5_
  32.9 40.0 %all-to-all-done = f32[64,6,4,128]{3,2,1,0:T(4,128)S(1)} async-done(((f32[64,6,4,128]{3,2,1,0:T(4,128)}), f32[64,6,4,128]{3,2,1,0:T(4,128)S(1)}, u32[]{:S(2)}, u32[]{:S(2)}) %all-to-all-start) | async-done | bytes 786464 | tf_op jit(solution)/shard_map/all_to_all | solution.py:316
  72.9 0.0 copy-done
  72.9 0.0 copy-done.1
  72.9 0.0 copy-done.2
  72.9 1.6 %pencil.1 = f32[384,128]{1,0:T(8,128)S(1)} custom-call(f32[1536,128]{1,0:T(8,128)S(1)} %bitcast.20, s32[1,1]{1,0:T(1,128)} %bitcast.2.refs_1_, f32[2,128,128]{2,1,0:T(8,128)S(1)} %copy-done, f32[2,128,128]{2,1,0:T(8,128)S(1)} %copy-done.1, f32[2,128,128]{2,1,0:T(8,128)S(1)} %copy-done.2, f32[64,128]{1,0:T(8,128)S(1)} %lines.1.refs_5_), custom_call_target="tpu_custom_call" | custom-call | flops 201326592 | bytes 1572864 | tf_op jit(solution)/shard_map/pencil/pallas_call | solution.py:397
  74.5 23.3 %all_to_all.15 = f32[64,3,2,128]{3,2,1,0:T(2,128)S(1)} all-to-all(f32[64,3,2,128]{3,2,1,0:T(2,128)S(1)} %bitcast.23), channel_id=1, replica_groups=mesh['lat'=64,'sec'=8] {'lat'}, dimensions={0} | all-to-all | bytes 393216 | tf_op jit(solution)/shard_map/all_to_all | solution.py:316
  97.8 0.6 owned.1
  98.4 7.9 %all-to-all-start.2 = ((f32[8,1,256]{2,1,0:T(1,128)}), f32[8,1,256]{2,1,0:T(1,128)S(1)}, u32[]{:S(2)}, u32[]{:S(2)}) async-start(f32[8,1,256]{2,1,0:T(1,128)} %owned.1), calls=%async_computation.2 | async-start | bytes 16384 | tf_op jit(solution)/shard_map/all_to_all | solution.py:417
  106.3 0.8 finish.1
  107.1 3.8 %all-to-all-done.2 = f32[8,1,256]{2,1,0:T(1,128)S(1)} async-done(((f32[8,1,256]{2,1,0:T(1,128)}), f32[8,1,256]{2,1,0:T(1,128)S(1)}, u32[]{:S(2)}, u32[]{:S(2)}) %all-to-all-start.2) | async-done | bytes 8224 | tf_op jit(solution)/shard_map/all_to_all | solution.py:417
  110.9 0.6 reduce_sum.11
  (1 shorter events, 0.0 us)
Async XLA Ops:
  1.9 10.3 %collective-permute-start = (f32[2,4,1024]{2,1,0:T(4,128)S(1)}, f32[2,4,1024]{2,1,0:T(4,128)S(1)}, u32[]{:S(2)}, u32[]{:S(2)}) collective-permute-start(f32[2,4,1024]{2,1,0:T(4,128)S(1)} %get-tuple-element.6), channel_id=1, source_target_pairs={{0,1},{1,2},{2,3},{3,4},{4,5},{5,6},{6,7},{8,9},{9,10},{10,11},{11... | collective-permute-start | bytes 98312 | tf_op jit(solution)/shard_map/ppermute | solution.py:310
  6.5 6.3 %collective-permute-start.1 = (f32[2,4,1024]{2,1,0:T(4,128)S(1)}, f32[2,4,1024]{2,1,0:T(4,128)S(1)}, u32[]{:S(2)}, u32[]{:S(2)}) collective-permute-start(f32[2,4,1024]{2,1,0:T(4,128)S(1)} %get-tuple-element.7), channel_id=1, source_target_pairs={{1,0},{2,1},{3,2},{4,3},{5,4},{6,5},{7,6},{9,8},{10,9},{11,10},{12... | collective-permute-start | bytes 98312 | tf_op jit(solution)/shard_map/ppermute | solution.py:310
  14.1 58.8 %copy-start = (f32[2,128,128]{2,1,0:T(8,128)S(1)}, f32[2,128,128]{2,1,0:T(8,128)}, u32[]{:S(2)}) copy-start(f32[2,128,128]{2,1,0:T(8,128)} %refs_2_.1) | copy-start | bytes 393220
  14.1 58.8 %copy-start.1 = (f32[2,128,128]{2,1,0:T(8,128)S(1)}, f32[2,128,128]{2,1,0:T(8,128)}, u32[]{:S(2)}) copy-start(f32[2,128,128]{2,1,0:T(8,128)} %refs_3_.1) | copy-start | bytes 393220
  14.1 58.8 %copy-start.2 = (f32[2,128,128]{2,1,0:T(8,128)S(1)}, f32[2,128,128]{2,1,0:T(8,128)}, u32[]{:S(2)}) copy-start(f32[2,128,128]{2,1,0:T(8,128)} %refs_4_.1) | copy-start | bytes 393220
  14.1 58.8 %all-to-all-start = ((f32[64,6,4,128]{3,2,1,0:T(4,128)}), f32[64,6,4,128]{3,2,1,0:T(4,128)S(1)}, u32[]{:S(2)}, u32[]{:S(2)}) async-start(f32[64,6,4,128]{3,2,1,0:T(4,128)} %bitcast), calls=%async_computation | async-start | bytes 1572864 | tf_op jit(solution)/shard_map/all_to_all | solution.py:316
  31.4 0.7 copy-start.4
  32.1 0.7 copy-start.3
  98.4 12.5 %all-to-all-start.2 = ((f32[8,1,256]{2,1,0:T(1,128)}), f32[8,1,256]{2,1,0:T(1,128)S(1)}, u32[]{:S(2)}, u32[]{:S(2)}) async-start(f32[8,1,256]{2,1,0:T(1,128)} %owned.1), calls=%async_computation.2 | async-start | bytes 16384 | tf_op jit(solution)/shard_map/all_to_all | solution.py:417

commit v2 on v1

v2 whole, which is shorter than its diff:
```python
import jax
import jax.numpy as jnp
from jax import lax
from jax.experimental import pallas as pl
from jax.experimental.pallas import tpu as pltpu
from jax.sharding import PartitionSpec as P

LANES = 128
ROWS = 8
WIDTH = LANES // ROWS
FIELDS = 5
FINITE_STEP = 0.03125
YIELD_WEIGHT = 0.25
HIGHEST = lax.Precision.HIGHEST
VMEM = pl.BlockSpec(memory_space=pltpu.VMEM)
HBM = pl.BlockSpec(memory_space=pltpu.HBM)
SMEM = pl.BlockSpec(memory_space=pltpu.SMEM)
MIB = 1024 * 1024


def places():
    row = lax.broadcasted_iota(jnp.int32, (ROWS, LANES), 0)
    lane = lax.broadcasted_iota(jnp.int32, (ROWS, LANES), 1)
    return row, lane // WIDTH, lane % WIDTH


def along_lane(block, row_of):
    return jnp.take_along_axis(block, row_of, axis=0, mode="promise_in_bounds")


def along_row(block, lane_of):
    return jnp.take_along_axis(block, lane_of, axis=1, mode="promise_in_bounds")


def to_lines(block, row_of):
    return along_lane(pltpu.roll(block, 0, 1, stride=WIDTH, stride_axis=0), row_of)


def tile_kernel(
    velocity_far,
    base_far,
    yielded_far,
    colors_far,
    forcing_far,
    lines,
    velocity,
    base,
    yielded,
    colors,
    forcing,
    landed,
):
    arrays = (
        (velocity_far, velocity),
        (base_far, base),
        (yielded_far, yielded),
        (colors_far, colors),
        (forcing_far, forcing),
    )
    copies = [pltpu.make_async_copy(far, near, landed.at[place]) for place, (far, near) in enumerate(arrays)]
    for copy in copies:
        copy.start()
    levels, _, width = velocity.shape
    blocks = width // LANES
    stride = lines.shape[0] // (blocks * ROWS)
    row, group, place = places()
    row_of = (group - row) & (ROWS - 1)
    lane = group * WIDTH + place
    kind = place // ROWS
    low_lane = (group * WIDTH - 1 - kind) & (LANES - 1)
    high_lane = (group * WIDTH + WIDTH + kind) & (LANES - 1)
    x_of = place & (ROWS - 1)
    sides = []
    for copy in copies[:3]:
        copy.wait()
    for level in range(levels):
        v = velocity[level]
        coef = yielded[level].astype(jnp.float32) * YIELD_WEIGHT
        eta = base[level] / (1.0 + coef * v * v)
        outer = []
        for block in range(blocks):
            span = slice(block * LANES, (block + 1) * LANES)
            here = eta[:, span]
            moved = jnp.where(place < ROWS, pltpu.roll(here, 1, 1), pltpu.roll(here, LANES - 1, 1))
            outer.append(jnp.where((place == 0) | (place == WIDTH - 1), v[:, span], moved))
        sides.append(outer)
    for copy in copies[3:]:
        copy.wait()
    for block in range(blocks):
        span = slice(block * LANES, (block + 1) * LANES)
        start = block * ROWS * stride
        rim = jnp.zeros((ROWS, LANES), jnp.float32)
        for level in range(levels):
            low = sides[level][block]
            high = low
            if block > 0:
                low = jnp.where(lane >= LANES - WIDTH, sides[level][block - 1], low)
            else:
                low = jnp.where(lane >= LANES - WIDTH, 0.0, low)
            if block < blocks - 1:
                high = jnp.where(lane < WIDTH, sides[level][block + 1], high)
            else:
                high = jnp.where(lane < WIDTH, 0.0, high)
            for side, picked in enumerate((along_row(low, low_lane), along_row(high, high_lane))):
                rim = jnp.where(row == 2 * level + side, along_lane(picked, x_of), rim)
            sent = (
                velocity[level, :, span],
                base[level, :, span],
                yielded[level, :, span].astype(jnp.float32) * YIELD_WEIGHT,
                FINITE_STEP * (colors[level, :, span] + 1).astype(jnp.float32),
                forcing[level, :, span],
            )
            for field, cells in enumerate(sent):
                lines[pl.ds(start + field * levels + level, ROWS, stride=stride), :] = to_lines(cells, row_of)
        rim = to_lines(rim, row_of)
        for spare in range(FIELDS * levels, stride):
            lines[pl.ds(start + spare, ROWS, stride=stride), :] = rim


def spread_rows(received, stride, field, levels, store):
    blocks = received.shape[0] // (stride * ROWS)
    for level in range(levels):
        for block in range(blocks):
            rows = received[pl.ds(block * ROWS * stride + field * levels + level, ROWS, stride=stride), :]
            store(block * ROWS * levels + level, rows)


def edge_kernel(levels, received, turn, velocity, viscosity, base, coef, low_edge, high_edge):
    radial = base.shape[0]
    stride = received.shape[0] * levels // radial
    nothing = jnp.zeros((ROWS, LANES), jnp.float32)
    for padded in (velocity, viscosity):
        padded[pl.ds(0, ROWS), :] = nothing
        padded[pl.ds(radial + ROWS, ROWS), :] = nothing

    def store_velocity(first, rows):
        velocity[pl.ds(ROWS + first, ROWS, stride=levels), :] = rows

    def store_base(first, rows):
        base[pl.ds(first, ROWS, stride=levels), :] = rows

    def store_coef(first, rows):
        coef[pl.ds(first, ROWS, stride=levels), :] = rows

    for field, store in enumerate((store_velocity, store_base, store_coef)):
        spread_rows(received, stride, field, levels, store)
    _, group, place = places()
    shift = turn[0, 0]
    first_lane = shift * WIDTH + place
    last_lane = ((shift + ROWS - 1) & (ROWS - 1)) * WIDTH + place
    for start in range(0, radial, ROWS):
        v = velocity[pl.ds(ROWS + start, ROWS), :]
        eta = base[pl.ds(start, ROWS), :] / (1.0 + coef[pl.ds(start, ROWS), :] * v * v)
        viscosity[pl.ds(ROWS + start, ROWS), :] = eta
        for kind, cells in enumerate((v, eta)):
            for edge, lane_of in ((low_edge, first_lane), (high_edge, last_lane)):
                edge[kind, pl.ds(start // ROWS, 1), :] = along_lane(along_row(cells, lane_of), group)[:1]


def middle_kernel(levels, received, turn, velocity, viscosity, base, coef, out, step, forcing):
    radial = base.shape[0]
    stride = received.shape[0] * levels // radial

    def store_step(first, rows):
        step[pl.ds(first, ROWS, stride=levels), :] = rows

    def store_forcing(first, rows):
        forcing[pl.ds(first, ROWS, stride=levels), :] = rows

    spread_rows(received, stride, 3, levels, store_step)
    spread_rows(received, stride, 4, levels, store_forcing)
    row, group, place = places()
    shift = turn[0, 0]
    x = (group - shift) & (ROWS - 1)
    first_x, last_x = x == 0, x == ROWS - 1
    first_y, last_y = place == 0, place == WIDTH - 1
    slot = 2 * (row % levels) + jnp.where(first_y, 0, 1)
    v_lane = ((slot + shift) & (ROWS - 1)) * WIDTH + x
    eta_lane = v_lane + ROWS

    def lateral(block, y_rim):
        return (
            jnp.where(first_x, 0.0, pltpu.roll(block, WIDTH, 1)),
            jnp.where(last_x, 0.0, pltpu.roll(block, LANES - WIDTH, 1)),
            jnp.where(first_y, y_rim, pltpu.roll(block, 1, 1)),
            jnp.where(last_y, y_rim, pltpu.roll(block, LANES - 1, 1)),
        )

    for start in range(0, radial, ROWS):
        here = pl.ds(start, ROWS)
        v = velocity[pl.ds(ROWS + start, ROWS), :]
        v_low = velocity[pl.ds(ROWS + start - 1, ROWS), :]
        v_high = velocity[pl.ds(ROWS + start + 1, ROWS), :]
        eta = viscosity[pl.ds(ROWS + start, ROWS), :]
        eta_low = viscosity[pl.ds(ROWS + start - 1, ROWS), :]
        eta_high = viscosity[pl.ds(ROWS + start + 1, ROWS), :]
        b = base[here, :]
        amount = coef[here, :]
        source = start // levels * stride + FIELDS * levels
        rim = received[pl.ds(source, 1), :]
        for later in range(1, ROWS // levels):
            rim = jnp.where(row < later * levels, rim, received[pl.ds(source + later * stride, 1), :])
        near_v = lateral(v, along_row(rim, v_lane)) + (v_low, v_high)
        near_eta = lateral(eta, along_row(rim, eta_lane)) + (eta_low, eta_high)
        value_sum = near_v[0]
        eta_sum = near_eta[0]
        product_sum = near_v[0] * near_eta[0]
        for near_value, near_visc in zip(near_v[1:], near_eta[1:]):
            value_sum = value_sum + near_value
            eta_sum = eta_sum + near_visc
            product_sum = product_sum + near_value * near_visc
        moved = v + step[here, :]
        moved_inverse = 1.0 / (1.0 + amount * moved * moved)
        moved_eta = b * moved_inverse
        slope = -amount * (moved + v) * eta * moved_inverse
        out[0, here, :] = value_sum
        out[1, here, :] = eta_sum
        out[2, here, :] = product_sum
        out[3, here, :] = slope
        out[4, here, :] = b * v - forcing[here, :]
        out[5, here, :] = 3.0 * moved_eta + b
        out[6, here, :] = 0.5 * (slope * (v_low - v) - eta_low - moved_eta)
        out[7, here, :] = 0.5 * (slope * (v_high - v) - eta_high - moved_eta)


def lines_kernel(line_ids, owner_ids, lines_of):
    entries = line_ids.shape[1]
    owner_count, line_count = lines_of.shape
    picks = (lax.broadcasted_iota(jnp.int32, (line_count, entries), 0) == line_ids[...]).astype(jnp.float32)
    owners = (lax.broadcasted_iota(jnp.int32, (owner_count, entries), 0) == owner_ids[...]).astype(jnp.float32)
    lines_of[...] = lax.dot_general(
        owners, picks, (((1,), (1,)), ((), ())), preferred_element_type=jnp.float32
    )


def pencil_kernel(
    levels,
    velocity,
    viscosity,
    middle,
    left,
    right,
    turn,
    block_diag,
    block_below,
    block_above,
    lines_of,
    out,
    work,
):
    radial = work.shape[1]
    devices = radial // levels
    row, group, place = places()
    x = (group - turn[0, 0]) & (ROWS - 1)
    first_x, last_x = x == 0, x == ROWS - 1
    own_lane = row * WIDTH + place

    def side(kind, start):
        low = along_row(jnp.broadcast_to(left[kind, pl.ds(start // ROWS, 1), :], (ROWS, LANES)), own_lane)
        high = along_row(jnp.broadcast_to(right[kind, pl.ds(start // ROWS, 1), :], (ROWS, LANES)), own_lane)
        return jnp.where(first_x, low, jnp.where(last_x, high, 0.0))

    for start in range(0, radial, ROWS):
        here = pl.ds(start, ROWS)
        v = velocity[pl.ds(ROWS + start, ROWS), :]
        eta = viscosity[pl.ds(ROWS + start, ROWS), :]
        v_rim = side(0, start)
        eta_rim = side(1, start)
        value_sum = middle[0, here, :] + v_rim
        eta_sum = middle[1, here, :] + eta_rim
        product_sum = middle[2, here, :] + v_rim * eta_rim
        spread = 6.0 * v - value_sum
        sensitivity = 0.5 * eta * spread
        work[0, here, :] = sensitivity + 0.5 * (v * eta_sum - product_sum) + middle[4, here, :]
        work[1, here, :] = 0.5 * eta_sum + 0.5 * middle[3, here, :] * spread + middle[5, here, :]
        work[2, here, :] = sensitivity

    residual = work[0]
    half = radial // 2

    def apply_blocks(field):
        head, tail = field[:half], field[half:]
        first = jnp.dot(block_diag[0], head, precision=HIGHEST, preferred_element_type=jnp.float32)
        first = first + jnp.dot(block_above[0], tail, precision=HIGHEST, preferred_element_type=jnp.float32)
        second = jnp.dot(block_diag[1], tail, precision=HIGHEST, preferred_element_type=jnp.float32)
        second = second + jnp.dot(block_below[1], head, precision=HIGHEST, preferred_element_type=jnp.float32)
        return jnp.concatenate([first, second], axis=0)

    initial = apply_blocks(residual)
    level_index = lax.broadcasted_iota(jnp.int32, (radial, LANES), 0)
    from_above = jnp.where(level_index == radial - 1, 0.0, pltpu.roll(middle[6] * initial, radial - 1, 0))
    from_below = jnp.where(level_index == 0, 0.0, pltpu.roll(middle[7] * initial, 1, 0))
    remainder = residual - (work[1] * initial + from_above + from_below)
    correction = initial + apply_blocks(remainder)
    gradient = correction * work[2]
    owned = lax.dot_general(
        lines_of[...],
        gradient,
        (((1,), (1,)), ((), ())),
        precision=HIGHEST,
        preferred_element_type=jnp.float32,
    )
    work[0] = correction
    parts = radial // LANES
    back = levels + parts
    for block in range(devices // ROWS):
        for level in range(levels):
            out[pl.ds(block * ROWS * back + level, ROWS, stride=back), :] = work[
                0, pl.ds(block * ROWS * levels + level, ROWS, stride=levels), :
            ]
        for part in range(parts):
            out[pl.ds(block * ROWS * back + levels + part, ROWS, stride=back), :] = owned[
                block * ROWS : (block + 1) * ROWS, part * LANES : (part + 1) * LANES
            ]


def owned_kernel(levels, received, owned):
    sectors, _, radial = owned.shape
    parts = radial // LANES
    back = levels + parts
    blocks = received.shape[0] // (back * ROWS)
    for part in range(parts):
        total = received[pl.ds(levels + part, ROWS, stride=back), :]
        for block in range(1, blocks):
            total = total + received[pl.ds(block * ROWS * back + levels + part, ROWS, stride=back), :]
        total = jnp.sum(total, axis=0, keepdims=True)
        for sector in range(sectors):
            owned[sector, :, part * LANES : (part + 1) * LANES] = total


def finish_kernel(received, correction):
    levels, rows, width = correction.shape
    blocks = width // LANES
    back = received.shape[0] // (blocks * ROWS)
    row, group, place = places()
    row_of = (group - row) & (ROWS - 1)
    lane_of = ((group + row) & (ROWS - 1)) * WIDTH + place
    for level in range(levels):
        for block in range(blocks):
            lines = received[pl.ds(block * ROWS * back + level, ROWS, stride=back), :]
            correction[level, :, block * LANES : (block + 1) * LANES] = along_row(
                along_lane(lines, row_of), lane_of
            )


def shifted(cells, axis, step):
    count = lax.axis_size(axis)
    return lax.ppermute(cells, axis, [(i, i + step) for i in range(count) if 0 <= i + step < count])


def swapped(rows, parts):
    devices = lax.axis_size("lat")
    sent = rows.reshape(devices, -1, parts, LANES)
    taken = lax.all_to_all(sent, "lat", split_axis=0, concat_axis=0, tiled=True)
    return taken.reshape(rows.shape)


def kernel_call(body, shapes, specs, work, name, scratch=()):
    return pl.pallas_call(
        body,
        out_shape=shapes,
        in_specs=specs,
        out_specs=[VMEM] * len(shapes),
        scratch_shapes=scratch,
        compiler_params=pltpu.CompilerParams(vmem_limit_bytes=32 * MIB),
        cost_estimate=pl.CostEstimate(flops=work[0], bytes_accessed=4 * work[1], transcendentals=0),
        name=name,
    )


def f32(*shape):
    return jax.ShapeDtypeStruct(shape, jnp.float32)


def local(
    velocity,
    base_visc,
    yielded,
    colors,
    forcing,
    block_diag,
    block_below,
    block_above,
    weak_lines,
    weak_owner,
):
    levels, rows, width = velocity.shape
    devices = lax.axis_size("lat")
    sectors = lax.axis_size("sec")
    radial = levels * devices
    cell_count = levels * rows * width
    tile = (levels, rows, width)
    sent_rows = FIELDS * levels + 2
    far = [
        pltpu.with_memory_space_constraint(array, pltpu.HBM)
        for array in (velocity, base_visc, yielded, colors, forcing)
    ]
    (lines,) = kernel_call(
        tile_kernel,
        [f32(devices * sent_rows, LANES)],
        [HBM] * FIELDS,
        (40 * cell_count, 12 * cell_count),
        "tile",
        [pltpu.VMEM(tile, array.dtype) for array in far]
        + [pltpu.SemaphoreType.DMA((FIELDS,))],
    )(*far)
    lines = swapped(lines, 2)

    picked = weak_lines.reshape(1, -1)
    turn = lax.axis_index("lat") & (rows - 1)
    place = (turn + picked // WIDTH) & (rows - 1)
    line_ids = place * WIDTH + picked % WIDTH
    (lines_of,) = kernel_call(
        lines_kernel,
        [f32(devices, LANES)],
        [VMEM] * 2,
        (2 * devices * LANES * 64, devices * LANES),
        "lines",
    )(line_ids, weak_owner.reshape(1, -1))
    back = levels + radial // LANES
    turn = turn.astype(jnp.int32).reshape(1, 1)
    padded = f32(radial + 2 * ROWS, LANES)
    whole = f32(radial, LANES)
    edge = f32(2, radial // ROWS, LANES)

    def edge_body(*refs):
        edge_kernel(levels, *refs)

    def middle_body(*refs):
        middle_kernel(levels, *refs)

    def pencil_body(*refs):
        pencil_kernel(levels, *refs)

    v, eta, base, coef, low_edge, high_edge = kernel_call(
        edge_body,
        [padded, padded, whole, whole, edge, edge],
        [VMEM, SMEM],
        (10 * cell_count, 7 * cell_count),
        "edges",
    )(lines, turn)
    left = shifted(high_edge, "sec", 1)
    right = shifted(low_edge, "sec", -1)
    (middle,) = kernel_call(
        middle_body,
        [f32(8, radial, LANES)],
        [VMEM, SMEM] + [VMEM] * 4,
        (60 * cell_count, 14 * cell_count),
        "middle",
        [pltpu.VMEM((radial, LANES), jnp.float32), pltpu.VMEM((radial, LANES), jnp.float32)],
    )(lines, turn, v, eta, base, coef)
    (improved,) = kernel_call(
        pencil_body,
        [f32(devices * back, LANES)],
        [VMEM] * 5 + [SMEM] + [VMEM] * 4,
        (24 * radial * radial * LANES, 12 * radial * LANES),
        "pencil",
        [pltpu.VMEM((3, radial, LANES), jnp.float32)],
    )(v, eta, middle, left, right, turn, block_diag, block_below, block_above, lines_of)
    improved = swapped(improved, 2)

    def owned_body(*refs):
        owned_kernel(levels, *refs)

    (owned,) = kernel_call(
        owned_body, [f32(sectors, 1, radial)], [VMEM], (devices * radial, devices * radial), "owned"
    )(improved)
    sums = lax.all_to_all(owned, "sec", split_axis=0, concat_axis=0, tiled=True)
    (correction,) = kernel_call(
        finish_kernel, [f32(*tile)], [VMEM], (4 * cell_count, 3 * cell_count), "finish"
    )(improved)
    weak_grad = jnp.sum(sums, axis=0)
    return (correction, weak_grad)


def solution(mesh):
    return jax.shard_map(
        local,
        mesh=mesh,
        in_specs=(
            P("lat", "sec", None),
            P("lat", "sec", None),
            P("lat", "sec", None),
            P("lat", "sec", None),
            P("lat", "sec", None),
            P(),
            P(),
            P(),
            P("sec", "lat", None),
            P("sec", "lat", None, None),
        ),
        out_specs=(P("lat", "sec", None), P("lat", None)),
        check_vma=False,
    )
```

time: 112 us -> 109 us (0.973)
  starting transfers between devices: 35.3 us -> 33.9 us
  waiting for transfers between devices: 44.4 us -> 43 us
    all_to_all x1, waiting for transfers between devices: 40 us -> 37.1 us  [swapped(): taken = lax.all_to_all(sent, 'lat', split_axis=0, concat_axis=0, tiled=True)]
    all_to_all x1, starting transfers between devices: 7.92 us -> 5.87 us  [local(): sums = lax.all_to_all(owned, 'sec', split_axis=0, concat_axis=0, tiled=True)]
    all_to_all x1, starting transfers between devices: 17.3 us -> 19.1 us  [swapped(): taken = lax.all_to_all(sent, 'lat', split_axis=0, concat_axis=0, tiled=True)]
    ppermute x2, waiting for transfers between devices: 0.59 us -> 1.99 us  [shifted(): lax.ppermute(cells, axis, [(i, i + step) for i in range(count) if 0 <= i...]
    ppermute x2, starting transfers between devices: 10.1 us -> 8.96 us  [shifted(): lax.ppermute(cells, axis, [(i, i + step) for i in range(count) if 0 <= i...]
where the time goes in v2:
time: 109 us; the launch traced here: 108 us
  waiting for transfers between devices  43 us (39%)
  starting transfers between devices  33.9 us (31%)
  blocking collectives  23.3 us (21%)
  Pallas kernels  6.21 us (6%)
    all_to_all x1, waiting for transfers between devices, swapped(): taken = lax.all_to_all(sent, 'lat', split_axis=0, concat_axis=0, tiled=True)  37.1 us
    all_to_all x1, blocking collectives, swapped(): taken = lax.all_to_all(sent, 'lat', split_axis=0, concat_axis=0, tiled=True)  23.3 us
    all_to_all x1, starting transfers between devices, swapped(): taken = lax.all_to_all(sent, 'lat', split_axis=0, concat_axis=0, tiled=True)  19.1 us
    ppermute x2, starting transfers between devices, shifted(): lax.ppermute(cells, axis, [(i, i + step) for i in range(count) if 0 <= i...  8.96 us
    all_to_all x1, starting transfers between devices, local(): sums = lax.all_to_all(owned, 'sec', split_axis=0, concat_axis=0, tiled=True)  5.87 us
    all_to_all x1, waiting for transfers between devices, local(): sums = lax.all_to_all(owned, 'sec', split_axis=0, concat_axis=0, tiled=True)  3.85 us
    pallas_call x1, Pallas kernels, local(): kernel_call(tile_kernel, [f32(devices * sent_rows, LANES)], [HBM] * FIELD...  2.79 us
  transfers between devices with their start and end apart: 4, of which 3 were waited for; matrix products, arithmetic and copies ran while one was open for 0% of the time, Pallas kernels for 1%

profile of v2, /device:TPU:1, one launch (start us, length us, event | category | flops | bytes accessed | tf_op | source)
XLA Modules:
  0.0 108.4 jit_solution(10264300035282843601)
XLA Ops:
  0.6 2.8 %tile.1 = f32[1408,128]{1,0:T(8,128)} custom-call(f32[4,8,1024]{2,1,0:T(8,128)} %velocity_far.1, f32[4,8,1024]{2,1,0:T(8,128)} %base_far.1, s32[4,8,1024]{2,1,0:T(8,128)} %yielded_far.1, s32[4,8,1024]{2,1,0:T(8,128)} %colors_far.1, f32[4,8,1024]{2,1,0:T(8,128)} %forcing_far.1), custom_call_target="tpu_custom_call" | custom-call | flops 1310720 | bytes 1572864 | tf_op jit(solution)/shard_map/tile/pallas_call | solution.py:398
  3.4 19.1 %all-to-all-start = ((f32[64,11,2,128]{3,2,1,0:T(2,128)}), f32[64,11,2,128]{3,2,1,0:T(2,128)S(1)}, u32[]{:S(2)}, u32[]{:S(2)}) async-start(f32[64,11,2,128]{3,2,1,0:T(2,128)} %bitcast), calls=%async_computation | async-start | bytes 1441792 | tf_op jit(solution)/shard_map/all_to_all | solution.py:354
  22.6 37.1 %all-to-all-done = f32[64,11,2,128]{3,2,1,0:T(2,128)S(1)} async-done(((f32[64,11,2,128]{3,2,1,0:T(2,128)}), f32[64,11,2,128]{3,2,1,0:T(2,128)S(1)}, u32[]{:S(2)}, u32[]{:S(2)}) %all-to-all-start) | async-done | bytes 720928 | tf_op jit(solution)/shard_map/all_to_all | solution.py:354
  59.7 0.2 edges.1
  59.9 0.0 copy-start.4
  59.9 7.0 %collective-permute-start = (f32[2,32,128]{2,1,0:T(8,128)S(1)}, f32[2,32,128]{2,1,0:T(8,128)S(1)}, u32[]{:S(2)}, u32[]{:S(2)}) collective-permute-start(f32[2,32,128]{2,1,0:T(8,128)S(1)} %get-tuple-element.12), channel_id=1, source_target_pairs={{0,1},{1,2},{2,3},{3,4},{4,5},{5,6},{6,7},{8,9},{9,10},{10,11},{11... | collective-permute-start | bytes 98312 | tf_op jit(solution)/shard_map/ppermute | solution.py:348
  67.0 1.9 %collective-permute-start.1 = (f32[2,32,128]{2,1,0:T(8,128)S(1)}, f32[2,32,128]{2,1,0:T(8,128)S(1)}, u32[]{:S(2)}, u32[]{:S(2)}) collective-permute-start(f32[2,32,128]{2,1,0:T(8,128)S(1)} %get-tuple-element.13), channel_id=1, source_target_pairs={{1,0},{2,1},{3,2},{4,3},{5,4},{6,5},{7,6},{9,8},{10,9},{11,10},{12... | collective-permute-start | bytes 98312 | tf_op jit(solution)/shard_map/ppermute | solution.py:348
  68.9 0.0 copy-done.4
  68.9 0.0 copy-start.3
  69.0 0.6 copy-done.3
  69.6 0.1 lines.1.refs_9_
  69.7 0.0 copy-start
  69.7 0.0 copy-start.1
  69.7 0.0 copy-start.2
  69.8 0.5 middle.1.refs_2_
  70.2 0.0 collective-permute-done.refs_3_
  70.2 2.0 %collective-permute-done.1.refs_4_ = f32[2,32,128]{2,1,0:T(8,128)S(1)} collective-permute-done((f32[2,32,128]{2,1,0:T(8,128)S(1)}, f32[2,32,128]{2,1,0:T(8,128)S(1)}, u32[]{:S(2)}, u32[]{:S(2)}) %collective-permute-start.1) | collective-permute-done | bytes 32800 | tf_op jit(solution)/shard_map/ppermute | solution.py:348
  72.2 0.0 copy-done
  72.2 0.0 copy-done.1
  72.2 0.0 copy-done.2
  72.2 1.2 %pencil.1 = f32[384,128]{1,0:T(8,128)S(1)} custom-call(f32[272,128]{1,0:T(8,128)S(1)} %get-tuple-element.8.refs_2_.refs_0_, f32[272,128]{1,0:T(8,128)S(1)} %get-tuple-element.9.refs_3_.refs_1_, f32[8,256,128]{2,1,0:T(8,128)S(1)} %middle.1.refs_2_, f32[2,32,128]{2,1,0:T(8,128)S(1)} %collective-permute-done.refs_3_, ...), custom_call_target="tpu_custom_call" | custom-call | flops 201326592 | bytes 1572864 | tf_op jit(solution)/shard_map/pencil/pallas_call | solution.py:452
  73.4 23.3 %all_to_all.15 = f32[64,3,2,128]{3,2,1,0:T(2,128)S(1)} all-to-all(f32[64,3,2,128]{3,2,1,0:T(2,128)S(1)} %bitcast.24), channel_id=1, replica_groups=mesh['lat'=64,'sec'=8] {'lat'}, dimensions={0} | all-to-all | bytes 393216 | tf_op jit(solution)/shard_map/all_to_all | solution.py:354
  96.8 0.6 owned.1
  97.4 5.9 %all-to-all-start.2 = ((f32[8,1,256]{2,1,0:T(1,128)}), f32[8,1,256]{2,1,0:T(1,128)S(1)}, u32[]{:S(2)}, u32[]{:S(2)}) async-start(f32[8,1,256]{2,1,0:T(1,128)} %owned.1), calls=%async_computation.2 | async-start | bytes 16384 | tf_op jit(solution)/shard_map/all_to_all | solution.py:468
  103.2 0.8 finish.1
  104.0 3.8 %all-to-all-done.2 = f32[8,1,256]{2,1,0:T(1,128)S(1)} async-done(((f32[8,1,256]{2,1,0:T(1,128)}), f32[8,1,256]{2,1,0:T(1,128)S(1)}, u32[]{:S(2)}, u32[]{:S(2)}) %all-to-all-start.2) | async-done | bytes 8224 | tf_op jit(solution)/shard_map/all_to_all | solution.py:468
  107.9 0.6 reduce_sum.11
  (1 shorter events, 0.0 us)
Async XLA Ops:
  3.4 56.3 %all-to-all-start = ((f32[64,11,2,128]{3,2,1,0:T(2,128)}), f32[64,11,2,128]{3,2,1,0:T(2,128)S(1)}, u32[]{:S(2)}, u32[]{:S(2)}) async-start(f32[64,11,2,128]{3,2,1,0:T(2,128)} %bitcast), calls=%async_computation | async-start | bytes 1441792 | tf_op jit(solution)/shard_map/all_to_all | solution.py:354
  59.9 9.0 %copy-start.4 = (s32[1,1,64]{2,1,0:T(1,128)S(1)}, s32[1,1,64]{2,1,0:T(1,128)}, u32[]{:S(2)}) copy-start(s32[1,1,64]{2,1,0:T(1,128)} %param.18) | copy-start | bytes 772
  59.9 10.3 %collective-permute-start = (f32[2,32,128]{2,1,0:T(8,128)S(1)}, f32[2,32,128]{2,1,0:T(8,128)S(1)}, u32[]{:S(2)}, u32[]{:S(2)}) collective-permute-start(f32[2,32,128]{2,1,0:T(8,128)S(1)} %get-tuple-element.12), channel_id=1, source_target_pairs={{0,1},{1,2},{2,3},{3,4},{4,5},{5,6},{6,7},{8,9},{9,10},{10,11},{11... | collective-permute-start | bytes 98312 | tf_op jit(solution)/shard_map/ppermute | solution.py:348
  67.0 5.2 %collective-permute-start.1 = (f32[2,32,128]{2,1,0:T(8,128)S(1)}, f32[2,32,128]{2,1,0:T(8,128)S(1)}, u32[]{:S(2)}, u32[]{:S(2)}) collective-permute-start(f32[2,32,128]{2,1,0:T(8,128)S(1)} %get-tuple-element.13), channel_id=1, source_target_pairs={{1,0},{2,1},{3,2},{4,3},{5,4},{6,5},{7,6},{9,8},{10,9},{11,10},{12... | collective-permute-start | bytes 98312 | tf_op jit(solution)/shard_map/ppermute | solution.py:348
  68.9 0.7 copy-start.3
  69.7 2.5 %copy-start = (f32[2,128,128]{2,1,0:T(8,128)S(1)}, f32[2,128,128]{2,1,0:T(8,128)}, u32[]{:S(2)}) copy-start(f32[2,128,128]{2,1,0:T(8,128)} %refs_6_.1) | copy-start | bytes 393220
  69.7 2.5 %copy-start.1 = (f32[2,128,128]{2,1,0:T(8,128)S(1)}, f32[2,128,128]{2,1,0:T(8,128)}, u32[]{:S(2)}) copy-start(f32[2,128,128]{2,1,0:T(8,128)} %refs_7_.1) | copy-start | bytes 393220
  69.7 2.5 %copy-start.2 = (f32[2,128,128]{2,1,0:T(8,128)S(1)}, f32[2,128,128]{2,1,0:T(8,128)}, u32[]{:S(2)}) copy-start(f32[2,128,128]{2,1,0:T(8,128)} %refs_8_.1) | copy-start | bytes 393220
  97.4 10.5 %all-to-all-start.2 = ((f32[8,1,256]{2,1,0:T(1,128)}), f32[8,1,256]{2,1,0:T(1,128)S(1)}, u32[]{:S(2)}, u32[]{:S(2)}) async-start(f32[8,1,256]{2,1,0:T(1,128)} %owned.1), calls=%async_computation.2 | async-start | bytes 16384 | tf_op jit(solution)/shard_map/all_to_all | solution.py:468

commit v3 on v2

--- a/solution.py
+++ b/solution.py
@@ -42,6 +42,7 @@
     yielded_far,
     colors_far,
     forcing_far,
+    lines_far,
     lines,
     velocity,
     base,
@@ -49,6 +50,7 @@
     colors,
     forcing,
     landed,
+    left,
 ):
     arrays = (
         (velocity_far, velocity),
@@ -86,6 +88,7 @@
         sides.append(outer)
     for copy in copies[3:]:
         copy.wait()
+    writes = []
     for block in range(blocks):
         span = slice(block * LANES, (block + 1) * LANES)
         start = block * ROWS * stride
@@ -113,8 +116,13 @@
             for field, cells in enumerate(sent):
                 lines[pl.ds(start + field * levels + level, ROWS, stride=stride), :] = to_lines(cells, row_of)
         rim = to_lines(rim, row_of)
-        for spare in range(FIELDS * levels, stride):
-            lines[pl.ds(start + spare, ROWS, stride=stride), :] = rim
+        lines[pl.ds(start + FIELDS * levels, ROWS, stride=stride), :] = rim
+        part = pl.ds(start, ROWS * stride)
+        copy = pltpu.make_async_copy(lines.at[part], lines_far.at[part], left.at[block])
+        copy.start()
+        writes.append(copy)
+    for copy in writes:
+        copy.wait()
 
 
 def spread_rows(received, stride, field, levels, store):
@@ -355,12 +363,12 @@
     return taken.reshape(rows.shape)
 
 
-def kernel_call(body, shapes, specs, work, name, scratch=()):
+def kernel_call(body, shapes, specs, work, name, scratch=(), into=VMEM):
     return pl.pallas_call(
         body,
         out_shape=shapes,
         in_specs=specs,
-        out_specs=[VMEM] * len(shapes),
+        out_specs=[into] * len(shapes),
         scratch_shapes=scratch,
         compiler_params=pltpu.CompilerParams(vmem_limit_bytes=32 * MIB),
         cost_estimate=pl.CostEstimate(flops=work[0], bytes_accessed=4 * work[1], transcendentals=0),
@@ -390,7 +398,7 @@
     radial = levels * devices
     cell_count = levels * rows * width
     tile = (levels, rows, width)
-    sent_rows = FIELDS * levels + 2
+    sent_rows = FIELDS * levels + 1
     far = [
         pltpu.with_memory_space_constraint(array, pltpu.HBM)
         for array in (velocity, base_visc, yielded, colors, forcing)
@@ -401,10 +409,12 @@
         [HBM] * FIELDS,
         (40 * cell_count, 12 * cell_count),
         "tile",
-        [pltpu.VMEM(tile, array.dtype) for array in far]
-        + [pltpu.SemaphoreType.DMA((FIELDS,))],
+        [pltpu.VMEM((devices * sent_rows, LANES), jnp.float32)]
+        + [pltpu.VMEM(tile, array.dtype) for array in far]
+        + [pltpu.SemaphoreType.DMA((FIELDS,)), pltpu.SemaphoreType.DMA((width // LANES,))],
+        HBM,
     )(*far)
-    lines = swapped(lines, 2)
+    lines = swapped(lines, 1)
 
     picked = weak_lines.reshape(1, -1)
     turn = lax.axis_index("lat") & (rows - 1)

time: 109 us -> 107 us (0.982)
  waiting for transfers between devices: 43 us -> 41.6 us
    all_to_all x1, waiting for transfers between devices: 37.1 us -> 35.8 us  [swapped(): taken = lax.all_to_all(sent, 'lat', split_axis=0, concat_axis=0, tiled=True)]
where the time goes in v3:
time: 107 us
  waiting for transfers between devices  41.6 us (39%)
  starting transfers between devices  33.9 us (32%)
  blocking collectives  23.3 us (22%)
  Pallas kernels  6.05 us (6%)
    all_to_all x1, waiting for transfers between devices, swapped(): taken = lax.all_to_all(sent, 'lat', split_axis=0, concat_axis=0, tiled=True)  35.8 us
    all_to_all x1, blocking collectives, swapped(): taken = lax.all_to_all(sent, 'lat', split_axis=0, concat_axis=0, tiled=True)  23.3 us
    all_to_all x1, starting transfers between devices, swapped(): taken = lax.all_to_all(sent, 'lat', split_axis=0, concat_axis=0, tiled=True)  19.1 us
    ppermute x2, starting transfers between devices, shifted(): lax.ppermute(cells, axis, [(i, i + step) for i in range(count) if 0 <= i...  8.96 us
    all_to_all x1, starting transfers between devices, local(): sums = lax.all_to_all(owned, 'sec', split_axis=0, concat_axis=0, tiled=True)  5.87 us
    all_to_all x1, waiting for transfers between devices, local(): sums = lax.all_to_all(owned, 'sec', split_axis=0, concat_axis=0, tiled=True)  3.85 us
    pallas_call x1, Pallas kernels, local(): kernel_call(tile_kernel, [f32(devices * sent_rows, LANES)], [HBM] * FIELD...  2.62 us
  transfers between devices with their start and end apart: 4, of which 3 were waited for; matrix products, arithmetic and copies ran while one was open for 0% of the time, Pallas kernels for 1%

profile of v3, /device:TPU:1, one launch (start us, length us, event | category | flops | bytes accessed | tf_op | source)
XLA Modules:
  0.0 106.9 jit_solution(2424733190568490508)
XLA Ops:
  0.6 2.6 %tile.1 = f32[1344,128]{1,0:T(8,128)} custom-call(f32[4,8,1024]{2,1,0:T(8,128)} %velocity_far.1, f32[4,8,1024]{2,1,0:T(8,128)} %base_far.1, s32[4,8,1024]{2,1,0:T(8,128)} %yielded_far.1, s32[4,8,1024]{2,1,0:T(8,128)} %colors_far.1, f32[4,8,1024]{2,1,0:T(8,128)} %forcing_far.1), custom_call_target="tpu_custom_call" | custom-call | flops 1310720 | bytes 1572864 | tf_op jit(solution)/shard_map/tile/pallas_call | solution.py:406
  3.3 19.1 %all-to-all-start = ((f32[64,21,1,128]{3,2,1,0:T(1,128)}), f32[64,21,1,128]{3,2,1,0:T(1,128)S(1)}, u32[]{:S(2)}, u32[]{:S(2)}) async-start(f32[64,21,1,128]{3,2,1,0:T(1,128)} %bitcast), calls=%async_computation | async-start | bytes 1376256 | tf_op jit(solution)/shard_map/all_to_all | solution.py:362
  22.4 35.8 %all-to-all-done = f32[64,21,1,128]{3,2,1,0:T(1,128)S(1)} async-done(((f32[64,21,1,128]{3,2,1,0:T(1,128)}), f32[64,21,1,128]{3,2,1,0:T(1,128)S(1)}, u32[]{:S(2)}, u32[]{:S(2)}) %all-to-all-start) | async-done | bytes 688160 | tf_op jit(solution)/shard_map/all_to_all | solution.py:362
  58.2 0.2 edges.1
  58.4 0.0 copy-start.4
  58.4 7.0 %collective-permute-start = (f32[2,32,128]{2,1,0:T(8,128)S(1)}, f32[2,32,128]{2,1,0:T(8,128)S(1)}, u32[]{:S(2)}, u32[]{:S(2)}) collective-permute-start(f32[2,32,128]{2,1,0:T(8,128)S(1)} %get-tuple-element.12), channel_id=1, source_target_pairs={{0,1},{1,2},{2,3},{3,4},{4,5},{5,6},{6,7},{8,9},{9,10},{10,11},{11... | collective-permute-start | bytes 98312 | tf_op jit(solution)/shard_map/ppermute | solution.py:356
  65.5 1.9 %collective-permute-start.1 = (f32[2,32,128]{2,1,0:T(8,128)S(1)}, f32[2,32,128]{2,1,0:T(8,128)S(1)}, u32[]{:S(2)}, u32[]{:S(2)}) collective-permute-start(f32[2,32,128]{2,1,0:T(8,128)S(1)} %get-tuple-element.13), channel_id=1, source_target_pairs={{1,0},{2,1},{3,2},{4,3},{5,4},{6,5},{7,6},{9,8},{10,9},{11,10},{12... | collective-permute-start | bytes 98312 | tf_op jit(solution)/shard_map/ppermute | solution.py:356
  67.4 0.0 copy-done.4
  67.4 0.0 copy-start.3
  67.4 0.6 copy-done.3
  68.1 0.1 lines.1.refs_9_
  68.2 0.0 copy-start
  68.2 0.0 copy-start.1
  68.2 0.0 copy-start.2
  68.2 0.5 middle.1.refs_2_
  68.7 0.0 collective-permute-done.refs_3_
  68.7 2.0 %collective-permute-done.1.refs_4_ = f32[2,32,128]{2,1,0:T(8,128)S(1)} collective-permute-done((f32[2,32,128]{2,1,0:T(8,128)S(1)}, f32[2,32,128]{2,1,0:T(8,128)S(1)}, u32[]{:S(2)}, u32[]{:S(2)}) %collective-permute-start.1) | collective-permute-done | bytes 32800 | tf_op jit(solution)/shard_map/ppermute | solution.py:356
  70.7 0.0 copy-done
  70.7 0.0 copy-done.1
  70.7 0.0 copy-done.2
  70.7 1.2 %pencil.1 = f32[384,128]{1,0:T(8,128)S(1)} custom-call(f32[272,128]{1,0:T(8,128)S(1)} %get-tuple-element.8.refs_2_.refs_0_, f32[272,128]{1,0:T(8,128)S(1)} %get-tuple-element.9.refs_3_.refs_1_, f32[8,256,128]{2,1,0:T(8,128)S(1)} %middle.1.refs_2_, f32[2,32,128]{2,1,0:T(8,128)S(1)} %collective-permute-done.refs_3_, ...), custom_call_target="tpu_custom_call" | custom-call | flops 201326592 | bytes 1572864 | tf_op jit(solution)/shard_map/pencil/pallas_call | solution.py:462
  71.9 23.3 %all_to_all.15 = f32[64,3,2,128]{3,2,1,0:T(2,128)S(1)} all-to-all(f32[64,3,2,128]{3,2,1,0:T(2,128)S(1)} %bitcast.24), channel_id=1, replica_groups=mesh['lat'=64,'sec'=8] {'lat'}, dimensions={0} | all-to-all | bytes 393216 | tf_op jit(solution)/shard_map/all_to_all | solution.py:362
  95.2 0.6 owned.1
  95.8 5.9 %all-to-all-start.2 = ((f32[8,1,256]{2,1,0:T(1,128)}), f32[8,1,256]{2,1,0:T(1,128)S(1)}, u32[]{:S(2)}, u32[]{:S(2)}) async-start(f32[8,1,256]{2,1,0:T(1,128)} %owned.1), calls=%async_computation.2 | async-start | bytes 16384 | tf_op jit(solution)/shard_map/all_to_all | solution.py:478
  101.7 0.8 finish.1
  102.5 3.8 %all-to-all-done.2 = f32[8,1,256]{2,1,0:T(1,128)S(1)} async-done(((f32[8,1,256]{2,1,0:T(1,128)}), f32[8,1,256]{2,1,0:T(1,128)S(1)}, u32[]{:S(2)}, u32[]{:S(2)}) %all-to-all-start.2) | async-done | bytes 8224 | tf_op jit(solution)/shard_map/all_to_all | solution.py:478
  106.3 0.6 reduce_sum.11
  (1 shorter events, 0.0 us)
Async XLA Ops:
  3.3 54.9 %all-to-all-start = ((f32[64,21,1,128]{3,2,1,0:T(1,128)}), f32[64,21,1,128]{3,2,1,0:T(1,128)S(1)}, u32[]{:S(2)}, u32[]{:S(2)}) async-start(f32[64,21,1,128]{3,2,1,0:T(1,128)} %bitcast), calls=%async_computation | async-start | bytes 1376256 | tf_op jit(solution)/shard_map/all_to_all | solution.py:362
  58.4 9.0 %copy-start.4 = (s32[1,1,64]{2,1,0:T(1,128)S(1)}, s32[1,1,64]{2,1,0:T(1,128)}, u32[]{:S(2)}) copy-start(s32[1,1,64]{2,1,0:T(1,128)} %param.18) | copy-start | bytes 772
  58.4 10.3 %collective-permute-start = (f32[2,32,128]{2,1,0:T(8,128)S(1)}, f32[2,32,128]{2,1,0:T(8,128)S(1)}, u32[]{:S(2)}, u32[]{:S(2)}) collective-permute-start(f32[2,32,128]{2,1,0:T(8,128)S(1)} %get-tuple-element.12), channel_id=1, source_target_pairs={{0,1},{1,2},{2,3},{3,4},{4,5},{5,6},{6,7},{8,9},{9,10},{10,11},{11... | collective-permute-start | bytes 98312 | tf_op jit(solution)/shard_map/ppermute | solution.py:356
  65.5 5.2 %collective-permute-start.1 = (f32[2,32,128]{2,1,0:T(8,128)S(1)}, f32[2,32,128]{2,1,0:T(8,128)S(1)}, u32[]{:S(2)}, u32[]{:S(2)}) collective-permute-start(f32[2,32,128]{2,1,0:T(8,128)S(1)} %get-tuple-element.13), channel_id=1, source_target_pairs={{1,0},{2,1},{3,2},{4,3},{5,4},{6,5},{7,6},{9,8},{10,9},{11,10},{12... | collective-permute-start | bytes 98312 | tf_op jit(solution)/shard_map/ppermute | solution.py:356
  67.4 0.7 copy-start.3
  68.2 2.5 %copy-start = (f32[2,128,128]{2,1,0:T(8,128)S(1)}, f32[2,128,128]{2,1,0:T(8,128)}, u32[]{:S(2)}) copy-start(f32[2,128,128]{2,1,0:T(8,128)} %refs_6_.1) | copy-start | bytes 393220
  68.2 2.5 %copy-start.1 = (f32[2,128,128]{2,1,0:T(8,128)S(1)}, f32[2,128,128]{2,1,0:T(8,128)}, u32[]{:S(2)}) copy-start(f32[2,128,128]{2,1,0:T(8,128)} %refs_7_.1) | copy-start | bytes 393220
  68.2 2.5 %copy-start.2 = (f32[2,128,128]{2,1,0:T(8,128)S(1)}, f32[2,128,128]{2,1,0:T(8,128)}, u32[]{:S(2)}) copy-start(f32[2,128,128]{2,1,0:T(8,128)} %refs_8_.1) | copy-start | bytes 393220
  95.8 10.5 %all-to-all-start.2 = ((f32[8,1,256]{2,1,0:T(1,128)}), f32[8,1,256]{2,1,0:T(1,128)S(1)}, u32[]{:S(2)}, u32[]{:S(2)}) async-start(f32[8,1,256]{2,1,0:T(1,128)} %owned.1), calls=%async_computation.2 | async-start | bytes 16384 | tf_op jit(solution)/shard_map/all_to_all | solution.py:478

commit v4 on v2

--- a/solution.py
+++ b/solution.py
@@ -14,7 +14,6 @@
 HIGHEST = lax.Precision.HIGHEST
 VMEM = pl.BlockSpec(memory_space=pltpu.VMEM)
 HBM = pl.BlockSpec(memory_space=pltpu.HBM)
-SMEM = pl.BlockSpec(memory_space=pltpu.SMEM)
 MIB = 1024 * 1024
 
 
@@ -113,8 +112,7 @@
             for field, cells in enumerate(sent):
                 lines[pl.ds(start + field * levels + level, ROWS, stride=stride), :] = to_lines(cells, row_of)
         rim = to_lines(rim, row_of)
-        for spare in range(FIELDS * levels, stride):
-            lines[pl.ds(start + spare, ROWS, stride=stride), :] = rim
+        lines[pl.ds(start + FIELDS * levels, ROWS, stride=stride), :] = rim
 
 
 def spread_rows(received, stride, field, levels, store):
@@ -125,7 +123,7 @@
             store(block * ROWS * levels + level, rows)
 
 
-def edge_kernel(levels, received, turn, velocity, viscosity, base, coef, low_edge, high_edge):
+def edge_kernel(levels, received, velocity, viscosity, base, coef, low_edge, high_edge):
     radial = base.shape[0]
     stride = received.shape[0] * levels // radial
     nothing = jnp.zeros((ROWS, LANES), jnp.float32)
@@ -145,7 +143,7 @@
     for field, store in enumerate((store_velocity, store_base, store_coef)):
         spread_rows(received, stride, field, levels, store)
     _, group, place = places()
-    shift = turn[0, 0]
+    shift = lax.axis_index("lat") & (ROWS - 1)
     first_lane = shift * WIDTH + place
     last_lane = ((shift + ROWS - 1) & (ROWS - 1)) * WIDTH + place
     for start in range(0, radial, ROWS):
@@ -157,7 +155,7 @@
                 edge[kind, pl.ds(start // ROWS, 1), :] = along_lane(along_row(cells, lane_of), group)[:1]
 
 
-def middle_kernel(levels, received, turn, velocity, viscosity, base, coef, out, step, forcing):
+def middle_kernel(levels, received, velocity, viscosity, base, coef, out, step, forcing):
     radial = base.shape[0]
     stride = received.shape[0] * levels // radial
 
@@ -170,7 +168,7 @@
     spread_rows(received, stride, 3, levels, store_step)
     spread_rows(received, stride, 4, levels, store_forcing)
     row, group, place = places()
-    shift = turn[0, 0]
+    shift = lax.axis_index("lat") & (ROWS - 1)
     x = (group - shift) & (ROWS - 1)
     first_x, last_x = x == 0, x == ROWS - 1
     first_y, last_y = place == 0, place == WIDTH - 1
@@ -226,7 +224,9 @@
 def lines_kernel(line_ids, owner_ids, lines_of):
     entries = line_ids.shape[1]
     owner_count, line_count = lines_of.shape
-    picks = (lax.broadcasted_iota(jnp.int32, (line_count, entries), 0) == line_ids[...]).astype(jnp.float32)
+    group = (line_ids[...] // WIDTH + lax.axis_index("lat")) & (ROWS - 1)
+    lane_of = group * WIDTH + line_ids[...] % WIDTH
+    picks = (lax.broadcasted_iota(jnp.int32, (line_count, entries), 0) == lane_of).astype(jnp.float32)
     owners = (lax.broadcasted_iota(jnp.int32, (owner_count, entries), 0) == owner_ids[...]).astype(jnp.float32)
     lines_of[...] = lax.dot_general(
         owners, picks, (((1,), (1,)), ((), ())), preferred_element_type=jnp.float32
@@ -240,7 +240,6 @@
     middle,
     left,
     right,
-    turn,
     block_diag,
     block_below,
     block_above,
@@ -251,7 +250,7 @@
     radial = work.shape[1]
     devices = radial // levels
     row, group, place = places()
-    x = (group - turn[0, 0]) & (ROWS - 1)
+    x = (group - lax.axis_index("lat")) & (ROWS - 1)
     first_x, last_x = x == 0, x == ROWS - 1
     own_lane = row * WIDTH + place
 
@@ -390,7 +389,7 @@
     radial = levels * devices
     cell_count = levels * rows * width
     tile = (levels, rows, width)
-    sent_rows = FIELDS * levels + 2
+    sent_rows = FIELDS * levels + 1
     far = [
         pltpu.with_memory_space_constraint(array, pltpu.HBM)
         for array in (velocity, base_visc, yielded, colors, forcing)
@@ -401,24 +400,18 @@
         [HBM] * FIELDS,
         (40 * cell_count, 12 * cell_count),
         "tile",
-        [pltpu.VMEM(tile, array.dtype) for array in far]
-        + [pltpu.SemaphoreType.DMA((FIELDS,))],
+        [pltpu.VMEM(tile, array.dtype) for array in far] + [pltpu.SemaphoreType.DMA((FIELDS,))],
     )(*far)
-    lines = swapped(lines, 2)
-
-    picked = weak_lines.reshape(1, -1)
-    turn = lax.axis_index("lat") & (rows - 1)
-    place = (turn + picked // WIDTH) & (rows - 1)
-    line_ids = place * WIDTH + picked % WIDTH
+    lines = swapped(lines, 1)
+
     (lines_of,) = kernel_call(
         lines_kernel,
         [f32(devices, LANES)],
         [VMEM] * 2,
         (2 * devices * LANES * 64, devices * LANES),
         "lines",
-    )(line_ids, weak_owner.reshape(1, -1))
+    )(weak_lines.reshape(1, -1), weak_owner.reshape(1, -1))
     back = levels + radial // LANES
-    turn = turn.astype(jnp.int32).reshape(1, 1)
     padded = f32(radial + 2 * ROWS, LANES)
     whole = f32(radial, LANES)
     edge = f32(2, radial // ROWS, LANES)
@@ -435,28 +428,28 @@
     v, eta, base, coef, low_edge, high_edge = kernel_call(
         edge_body,
         [padded, padded, whole, whole, edge, edge],
-        [VMEM, SMEM],
+        [VMEM],
         (10 * cell_count, 7 * cell_count),
         "edges",
-    )(lines, turn)
+    )(lines)
     left = shifted(high_edge, "sec", 1)
     right = shifted(low_edge, "sec", -1)
     (middle,) = kernel_call(
         middle_body,
         [f32(8, radial, LANES)],
-        [VMEM, SMEM] + [VMEM] * 4,
+        [VMEM] * 5,
         (60 * cell_count, 14 * cell_count),
         "middle",
         [pltpu.VMEM((radial, LANES), jnp.float32), pltpu.VMEM((radial, LANES), jnp.float32)],
-    )(lines, turn, v, eta, base, coef)
+    )(lines, v, eta, base, coef)
     (improved,) = kernel_call(
         pencil_body,
         [f32(devices * back, LANES)],
-        [VMEM] * 5 + [SMEM] + [VMEM] * 4,
+        [VMEM] * 9,
         (24 * radial * radial * LANES, 12 * radial * LANES),
         "pencil",
         [pltpu.VMEM((3, radial, LANES), jnp.float32)],
-    )(v, eta, middle, left, right, turn, block_diag, block_below, block_above, lines_of)
+    )(v, eta, middle, left, right, block_diag, block_below, block_above, lines_of)
     improved = swapped(improved, 2)
 
     def owned_body(*refs):

time: 109 us -> 106 us (0.972)
  blocking collectives: 23.3 us -> 78 us
  waiting for transfers between devices: 43 us -> 5.83 us
  starting transfers between devices: 33.9 us -> 14.8 us
    all_to_all x1 -> x2, blocking collectives: 23.3 us -> 78 us  [swapped(): taken = lax.all_to_all(sent, 'lat', split_axis=0, concat_axis=0, tiled=True)]
    all_to_all x1 -> x0, waiting for transfers between devices: 37.1 us -> none  [swapped(): taken = lax.all_to_all(sent, 'lat', split_axis=0, concat_axis=0, tiled=True)]
    all_to_all x1 -> x0, starting transfers between devices: 19.1 us -> none  [swapped(): taken = lax.all_to_all(sent, 'lat', split_axis=0, concat_axis=0, tiled=True)]
  transfers between devices with their start and end apart: 4 -> 3, of which waited for: 3 -> 2; matrix products, arithmetic and copies ran while one was open for 0% -> 0% of each run, Pallas kernels for 1% -> 1%
where the time goes in v4:
time: 106 us
  blocking collectives  78 us (74%)
  starting transfers between devices  14.8 us (14%)
  waiting for transfers between devices  5.83 us (6%)
  Pallas kernels  5.35 us (5%)
    all_to_all x2, blocking collectives, swapped(): taken = lax.all_to_all(sent, 'lat', split_axis=0, concat_axis=0, tiled=True)  78 us
    ppermute x2, starting transfers between devices, shifted(): lax.ppermute(cells, axis, [(i, i + step) for i in range(count) if 0 <= i...  8.96 us
    all_to_all x1, starting transfers between devices, local(): sums = lax.all_to_all(owned, 'sec', split_axis=0, concat_axis=0, tiled=True)  5.87 us
    all_to_all x1, waiting for transfers between devices, local(): sums = lax.all_to_all(owned, 'sec', split_axis=0, concat_axis=0, tiled=True)  3.85 us
  transfers between devices with their start and end apart: 3, of which 2 were waited for; matrix products, arithmetic and copies ran while one was open for 0% of the time, Pallas kernels for 1%

profile of v4, /device:TPU:1, one launch (start us, length us, event | category | flops | bytes accessed | tf_op | source)
XLA Modules:
  0.0 106.0 jit_solution(10413441055490743670)
XLA Ops:
  0.6 1.9 %tile.1 = f32[1344,128]{1,0:T(8,128)S(1)} custom-call(f32[4,8,1024]{2,1,0:T(8,128)} %velocity_far.1, f32[4,8,1024]{2,1,0:T(8,128)} %base_far.1, s32[4,8,1024]{2,1,0:T(8,128)} %yielded_far.1, s32[4,8,1024]{2,1,0:T(8,128)} %colors_far.1, f32[4,8,1024]{2,1,0:T(8,128)} %forcing_far.1), custom_call_target="tpu_custom_call" | custom-call | flops 1310720 | bytes 1572864 | tf_op jit(solution)/shard_map/tile/pallas_call | solution.py:397
  2.6 54.7 %all_to_all.15 = f32[64,21,1,128]{3,2,1,0:T(1,128)S(1)} all-to-all(f32[64,21,1,128]{3,2,1,0:T(1,128)S(1)} %bitcast.9), channel_id=1, replica_groups=mesh['lat'=64,'sec'=8] {'lat'}, dimensions={0} | all-to-all | bytes 1376256 | tf_op jit(solution)/shard_map/all_to_all | solution.py:353
  57.2 0.2 edges.1
  57.5 7.0 %collective-permute-start = (f32[2,32,128]{2,1,0:T(8,128)S(1)}, f32[2,32,128]{2,1,0:T(8,128)S(1)}, u32[]{:S(2)}, u32[]{:S(2)}) collective-permute-start(f32[2,32,128]{2,1,0:T(8,128)S(1)} %get-tuple-element.12), channel_id=1, source_target_pairs={{0,1},{1,2},{2,3},{3,4},{4,5},{5,6},{6,7},{8,9},{9,10},{10,11},{11... | collective-permute-start | bytes 98312 | tf_op jit(solution)/shard_map/ppermute | solution.py:347
  64.5 1.9 %collective-permute-start.1 = (f32[2,32,128]{2,1,0:T(8,128)S(1)}, f32[2,32,128]{2,1,0:T(8,128)S(1)}, u32[]{:S(2)}, u32[]{:S(2)}) collective-permute-start(f32[2,32,128]{2,1,0:T(8,128)S(1)} %get-tuple-element.13), channel_id=1, source_target_pairs={{1,0},{2,1},{3,2},{4,3},{5,4},{6,5},{7,6},{9,8},{10,9},{11,10},{12... | collective-permute-start | bytes 98312 | tf_op jit(solution)/shard_map/ppermute | solution.py:347
  66.5 0.0 copy-start.3
  66.5 0.0 copy-start.4
  66.5 0.6 copy-done.3
  67.1 0.0 copy-done.4
  67.1 0.1 lines.1.refs_8_
  67.3 0.0 copy-start
  67.3 0.0 copy-start.1
  67.3 0.0 copy-start.2
  67.3 0.5 middle.1.refs_2_
  67.8 0.0 collective-permute-done.refs_3_
  67.8 2.0 %collective-permute-done.1.refs_4_ = f32[2,32,128]{2,1,0:T(8,128)S(1)} collective-permute-done((f32[2,32,128]{2,1,0:T(8,128)S(1)}, f32[2,32,128]{2,1,0:T(8,128)S(1)}, u32[]{:S(2)}, u32[]{:S(2)}) %collective-permute-start.1) | collective-permute-done | bytes 32800 | tf_op jit(solution)/shard_map/ppermute | solution.py:347
  69.8 0.0 copy-done
  69.8 0.0 copy-done.1
  69.8 0.0 copy-done.2
  69.8 1.2 %pencil.1 = f32[384,128]{1,0:T(8,128)S(1)} custom-call(f32[272,128]{1,0:T(8,128)S(1)} %get-tuple-element.8.refs_1_.refs_0_, f32[272,128]{1,0:T(8,128)S(1)} %get-tuple-element.9.refs_2_.refs_1_, f32[8,256,128]{2,1,0:T(8,128)S(1)} %middle.1.refs_2_, f32[2,32,128]{2,1,0:T(8,128)S(1)} %collective-permute-done.refs_3_, ...), custom_call_target="tpu_custom_call" | custom-call | flops 201326592 | bytes 1572864 | tf_op jit(solution)/shard_map/pencil/pallas_call | solution.py:445
  71.0 23.3 %all_to_all.16 = f32[64,3,2,128]{3,2,1,0:T(2,128)S(1)} all-to-all(f32[64,3,2,128]{3,2,1,0:T(2,128)S(1)} %bitcast.12), channel_id=1, replica_groups=mesh['lat'=64,'sec'=8] {'lat'}, dimensions={0} | all-to-all | bytes 393216 | tf_op jit(solution)/shard_map/all_to_all | solution.py:353
  94.3 0.6 owned.1
  94.9 5.9 %all-to-all-start.2 = ((f32[8,1,256]{2,1,0:T(1,128)}), f32[8,1,256]{2,1,0:T(1,128)S(1)}, u32[]{:S(2)}, u32[]{:S(2)}) async-start(f32[8,1,256]{2,1,0:T(1,128)} %owned.1), calls=%async_computation.2 | async-start | bytes 16384 | tf_op jit(solution)/shard_map/all_to_all | solution.py:461
  100.8 0.8 finish.1
  101.5 3.8 %all-to-all-done.2 = f32[8,1,256]{2,1,0:T(1,128)S(1)} async-done(((f32[8,1,256]{2,1,0:T(1,128)}), f32[8,1,256]{2,1,0:T(1,128)S(1)}, u32[]{:S(2)}, u32[]{:S(2)}) %all-to-all-start.2) | async-done | bytes 8224 | tf_op jit(solution)/shard_map/all_to_all | solution.py:461
  105.4 0.6 reduce_sum.11
Async XLA Ops:
  57.5 10.3 %collective-permute-start = (f32[2,32,128]{2,1,0:T(8,128)S(1)}, f32[2,32,128]{2,1,0:T(8,128)S(1)}, u32[]{:S(2)}, u32[]{:S(2)}) collective-permute-start(f32[2,32,128]{2,1,0:T(8,128)S(1)} %get-tuple-element.12), channel_id=1, source_target_pairs={{0,1},{1,2},{2,3},{3,4},{4,5},{5,6},{6,7},{8,9},{9,10},{10,11},{11... | collective-permute-start | bytes 98312 | tf_op jit(solution)/shard_map/ppermute | solution.py:347
  64.5 5.2 %collective-permute-start.1 = (f32[2,32,128]{2,1,0:T(8,128)S(1)}, f32[2,32,128]{2,1,0:T(8,128)S(1)}, u32[]{:S(2)}, u32[]{:S(2)}) collective-permute-start(f32[2,32,128]{2,1,0:T(8,128)S(1)} %get-tuple-element.13), channel_id=1, source_target_pairs={{1,0},{2,1},{3,2},{4,3},{5,4},{6,5},{7,6},{9,8},{10,9},{11,10},{12... | collective-permute-start | bytes 98312 | tf_op jit(solution)/shard_map/ppermute | solution.py:347
  66.5 0.7 copy-start.3
  66.5 0.7 copy-start.4
  67.3 2.5 %copy-start = (f32[2,128,128]{2,1,0:T(8,128)S(1)}, f32[2,128,128]{2,1,0:T(8,128)}, u32[]{:S(2)}) copy-start(f32[2,128,128]{2,1,0:T(8,128)} %refs_5_.1) | copy-start | bytes 393220
  67.3 2.5 %copy-start.1 = (f32[2,128,128]{2,1,0:T(8,128)S(1)}, f32[2,128,128]{2,1,0:T(8,128)}, u32[]{:S(2)}) copy-start(f32[2,128,128]{2,1,0:T(8,128)} %refs_6_.1) | copy-start | bytes 393220
  67.3 2.5 %copy-start.2 = (f32[2,128,128]{2,1,0:T(8,128)S(1)}, f32[2,128,128]{2,1,0:T(8,128)}, u32[]{:S(2)}) copy-start(f32[2,128,128]{2,1,0:T(8,128)} %refs_7_.1) | copy-start | bytes 393220
  94.9 10.5 %all-to-all-start.2 = ((f32[8,1,256]{2,1,0:T(1,128)}), f32[8,1,256]{2,1,0:T(1,128)S(1)}, u32[]{:S(2)}, u32[]{:S(2)}) async-start(f32[8,1,256]{2,1,0:T(1,128)} %owned.1), calls=%async_computation.2 | async-start | bytes 16384 | tf_op jit(solution)/shard_map/all_to_all | solution.py:461

commit v5 on v4

--- a/solution.py
+++ b/solution.py
@@ -11,7 +11,6 @@
 FIELDS = 5
 FINITE_STEP = 0.03125
 YIELD_WEIGHT = 0.25
-HIGHEST = lax.Precision.HIGHEST
 VMEM = pl.BlockSpec(memory_space=pltpu.VMEM)
 HBM = pl.BlockSpec(memory_space=pltpu.HBM)
 MIB = 1024 * 1024
@@ -221,16 +220,33 @@
         out[7, here, :] = 0.5 * (slope * (v_high - v) - eta_high - moved_eta)
 
 
-def lines_kernel(line_ids, owner_ids, lines_of):
+def halves(wide):
+    high = wide.astype(jnp.bfloat16)
+    return high, (wide - high.astype(jnp.float32)).astype(jnp.bfloat16)
+
+
+def product(left, right, dims):
+    return lax.dot_general(left, right, (dims, ((), ())), preferred_element_type=jnp.float32)
+
+
+def lines_kernel(line_ids, owner_ids, block_diag, block_below, block_above, lines_of, high, low):
     entries = line_ids.shape[1]
     owner_count, line_count = lines_of.shape
     group = (line_ids[...] // WIDTH + lax.axis_index("lat")) & (ROWS - 1)
     lane_of = group * WIDTH + line_ids[...] % WIDTH
-    picks = (lax.broadcasted_iota(jnp.int32, (line_count, entries), 0) == lane_of).astype(jnp.float32)
-    owners = (lax.broadcasted_iota(jnp.int32, (owner_count, entries), 0) == owner_ids[...]).astype(jnp.float32)
-    lines_of[...] = lax.dot_general(
-        owners, picks, (((1,), (1,)), ((), ())), preferred_element_type=jnp.float32
+    picks = (lax.broadcasted_iota(jnp.int32, (line_count, entries), 0) == lane_of).astype(jnp.bfloat16)
+    owners = (lax.broadcasted_iota(jnp.int32, (owner_count, entries), 0) == owner_ids[...]).astype(jnp.bfloat16)
+    lines_of[...] = product(owners, picks, ((1,), (1,))).astype(jnp.bfloat16)
+    half = block_diag.shape[1]
+    quarters = (
+        (0, 0, block_diag[0]),
+        (0, half, block_above[0]),
+        (half, 0, block_below[1]),
+        (half, half, block_diag[1]),
     )
+    for first_row, first_column, block in quarters:
+        place = (pl.ds(first_row, half), pl.ds(first_column, half))
+        high[place], low[place] = halves(block)
 
 
 def pencil_kernel(
@@ -240,9 +256,8 @@
     middle,
     left,
     right,
-    block_diag,
-    block_below,
-    block_above,
+    blocks_high,
+    blocks_low,
     lines_of,
     out,
     work,
@@ -275,15 +290,12 @@
         work[2, here, :] = sensitivity
 
     residual = work[0]
-    half = radial // 2
+    whole = ((1,), (0,))
 
     def apply_blocks(field):
-        head, tail = field[:half], field[half:]
-        first = jnp.dot(block_diag[0], head, precision=HIGHEST, preferred_element_type=jnp.float32)
-        first = first + jnp.dot(block_above[0], tail, precision=HIGHEST, preferred_element_type=jnp.float32)
-        second = jnp.dot(block_diag[1], tail, precision=HIGHEST, preferred_element_type=jnp.float32)
-        second = second + jnp.dot(block_below[1], head, precision=HIGHEST, preferred_element_type=jnp.float32)
-        return jnp.concatenate([first, second], axis=0)
+        high, low = halves(field)
+        small = product(blocks_high[...], low, whole) + product(blocks_low[...], high, whole)
+        return small + product(blocks_high[...], high, whole)
 
     initial = apply_blocks(residual)
     level_index = lax.broadcasted_iota(jnp.int32, (radial, LANES), 0)
@@ -292,13 +304,9 @@
     remainder = residual - (work[1] * initial + from_above + from_below)
     correction = initial + apply_blocks(remainder)
     gradient = correction * work[2]
-    owned = lax.dot_general(
-        lines_of[...],
-        gradient,
-        (((1,), (1,)), ((), ())),
-        precision=HIGHEST,
-        preferred_element_type=jnp.float32,
-    )
+    high, low = halves(gradient)
+    over_lines = ((1,), (1,))
+    owned = product(lines_of[...], low, over_lines) + product(lines_of[...], high, over_lines)
     work[0] = correction
     parts = radial // LANES
     back = levels + parts
@@ -404,13 +412,16 @@
     )(*far)
     lines = swapped(lines, 1)
 
-    (lines_of,) = kernel_call(
+    def b16(*shape):
+        return jax.ShapeDtypeStruct(shape, jnp.bfloat16)
+
+    lines_of, blocks_high, blocks_low = kernel_call(
         lines_kernel,
-        [f32(devices, LANES)],
-        [VMEM] * 2,
-        (2 * devices * LANES * 64, devices * LANES),
+        [b16(devices, LANES), b16(radial, radial), b16(radial, radial)],
+        [VMEM] * 5,
+        (2 * devices * LANES * 64, 3 * radial * radial),
         "lines",
-    )(weak_lines.reshape(1, -1), weak_owner.reshape(1, -1))
+    )(weak_lines.reshape(1, -1), weak_owner.reshape(1, -1), block_diag, block_below, block_above)
     back = levels + radial // LANES
     padded = f32(radial + 2 * ROWS, LANES)
     whole = f32(radial, LANES)
@@ -445,11 +456,11 @@
     (improved,) = kernel_call(
         pencil_body,
         [f32(devices * back, LANES)],
-        [VMEM] * 9,
+        [VMEM] * 8,
         (24 * radial * radial * LANES, 12 * radial * LANES),
         "pencil",
         [pltpu.VMEM((3, radial, LANES), jnp.float32)],
-    )(v, eta, middle, left, right, block_diag, block_below, block_above, lines_of)
+    )(v, eta, middle, left, right, blocks_high, blocks_low, lines_of)
     improved = swapped(improved, 2)
 
     def owned_body(*refs):

time: 106 us -> 106 us (level)
  no operation moved by 1% of the time
where the time goes in v5:
time: 106 us; the launch traced here: 105 us
  blocking collectives  78 us (74%)
  starting transfers between devices  14.6 us (14%)
  waiting for transfers between devices  5.84 us (6%)
  Pallas kernels  5.1 us (5%)
    all_to_all x2, blocking collectives, swapped(): taken = lax.all_to_all(sent, 'lat', split_axis=0, concat_axis=0, tiled=True)  78 us
    ppermute x2, starting transfers between devices, shifted(): lax.ppermute(cells, axis, [(i, i + step) for i in range(count) if 0 <= i...  8.96 us
    all_to_all x1, starting transfers between devices, local(): sums = lax.all_to_all(owned, 'sec', split_axis=0, concat_axis=0, tiled=True)  5.63 us
    all_to_all x1, waiting for transfers between devices, local(): sums = lax.all_to_all(owned, 'sec', split_axis=0, concat_axis=0, tiled=True)  3.85 us
  transfers between devices with their start and end apart: 3, of which 2 were waited for; matrix products, arithmetic and copies ran while one was open for 0% of the time, Pallas kernels for 1%

profile of v5, /device:TPU:1, one launch (start us, length us, event | category | flops | bytes accessed | tf_op | source)
XLA Modules:
  0.0 105.5 jit_solution(17047464856033772902)
XLA Ops:
  0.6 1.9 %tile.1 = f32[1344,128]{1,0:T(8,128)S(1)} custom-call(f32[4,8,1024]{2,1,0:T(8,128)} %velocity_far.1, f32[4,8,1024]{2,1,0:T(8,128)} %base_far.1, s32[4,8,1024]{2,1,0:T(8,128)} %yielded_far.1, s32[4,8,1024]{2,1,0:T(8,128)} %colors_far.1, f32[4,8,1024]{2,1,0:T(8,128)} %forcing_far.1), custom_call_target="tpu_custom_call" | custom-call | flops 1310720 | bytes 1572864 | tf_op jit(solution)/shard_map/tile/pallas_call | solution.py:405
  2.6 54.7 %all_to_all.15 = f32[64,21,1,128]{3,2,1,0:T(1,128)S(1)} all-to-all(f32[64,21,1,128]{3,2,1,0:T(1,128)S(1)} %bitcast.9), channel_id=1, replica_groups=mesh['lat'=64,'sec'=8] {'lat'}, dimensions={0} | all-to-all | bytes 1376256 | tf_op jit(solution)/shard_map/all_to_all | solution.py:361
  57.2 0.0 copy-start
  57.2 0.0 copy-start.1
  57.2 0.0 copy-start.2
  57.2 0.2 edges.1
  57.5 7.0 %collective-permute-start = (f32[2,32,128]{2,1,0:T(8,128)S(1)}, f32[2,32,128]{2,1,0:T(8,128)S(1)}, u32[]{:S(2)}, u32[]{:S(2)}) collective-permute-start(f32[2,32,128]{2,1,0:T(8,128)S(1)} %get-tuple-element.15), channel_id=1, source_target_pairs={{0,1},{1,2},{2,3},{3,4},{4,5},{5,6},{6,7},{8,9},{9,10},{10,11},{11... | collective-permute-start | bytes 98312 | tf_op jit(solution)/shard_map/ppermute | solution.py:355
  64.5 1.9 %collective-permute-start.1 = (f32[2,32,128]{2,1,0:T(8,128)S(1)}, f32[2,32,128]{2,1,0:T(8,128)S(1)}, u32[]{:S(2)}, u32[]{:S(2)}) collective-permute-start(f32[2,32,128]{2,1,0:T(8,128)S(1)} %get-tuple-element.16), channel_id=1, source_target_pairs={{1,0},{2,1},{3,2},{4,3},{5,4},{6,5},{7,6},{9,8},{10,9},{11,10},{12... | collective-permute-start | bytes 98312 | tf_op jit(solution)/shard_map/ppermute | solution.py:355
  66.5 0.0 copy-start.3
  66.5 0.0 copy-start.4
  66.5 0.0 copy-done
  66.5 0.0 copy-done.1
  66.5 0.0 copy-done.2
  66.5 0.6 copy-done.3
  67.1 0.0 copy-done.4
  67.1 0.2 lines.1
  67.3 0.5 middle.1.refs_2_
  67.8 0.0 collective-permute-done.refs_3_
  67.8 2.0 %collective-permute-done.1.refs_4_ = f32[2,32,128]{2,1,0:T(8,128)S(1)} collective-permute-done((f32[2,32,128]{2,1,0:T(8,128)S(1)}, f32[2,32,128]{2,1,0:T(8,128)S(1)}, u32[]{:S(2)}, u32[]{:S(2)}) %collective-permute-start.1) | collective-permute-done | bytes 32800 | tf_op jit(solution)/shard_map/ppermute | solution.py:355
  69.8 0.9 pencil.1
  70.7 23.3 %all_to_all.16 = f32[64,3,2,128]{3,2,1,0:T(2,128)S(1)} all-to-all(f32[64,3,2,128]{3,2,1,0:T(2,128)S(1)} %bitcast.12), channel_id=1, replica_groups=mesh['lat'=64,'sec'=8] {'lat'}, dimensions={0} | all-to-all | bytes 393216 | tf_op jit(solution)/shard_map/all_to_all | solution.py:361
  94.0 0.6 owned.1
  94.6 5.6 %all-to-all-start.2 = ((f32[8,1,256]{2,1,0:T(1,128)}), f32[8,1,256]{2,1,0:T(1,128)S(1)}, u32[]{:S(2)}, u32[]{:S(2)}) async-start(f32[8,1,256]{2,1,0:T(1,128)} %owned.1), calls=%async_computation.2 | async-start | bytes 16384 | tf_op jit(solution)/shard_map/all_to_all | solution.py:472
  100.3 0.8 finish.1
  101.0 3.8 %all-to-all-done.2 = f32[8,1,256]{2,1,0:T(1,128)S(1)} async-done(((f32[8,1,256]{2,1,0:T(1,128)}), f32[8,1,256]{2,1,0:T(1,128)S(1)}, u32[]{:S(2)}, u32[]{:S(2)}) %all-to-all-start.2) | async-done | bytes 8224 | tf_op jit(solution)/shard_map/all_to_all | solution.py:472
  104.9 0.6 reduce_sum.11
Async XLA Ops:
  57.2 9.3 %copy-start = (f32[2,128,128]{2,1,0:T(8,128)S(1)}, f32[2,128,128]{2,1,0:T(8,128)}, u32[]{:S(2)}) copy-start(f32[2,128,128]{2,1,0:T(8,128)} %block_diag.1) | copy-start | bytes 393220
  57.2 9.3 %copy-start.1 = (f32[2,128,128]{2,1,0:T(8,128)S(1)}, f32[2,128,128]{2,1,0:T(8,128)}, u32[]{:S(2)}) copy-start(f32[2,128,128]{2,1,0:T(8,128)} %block_below.1) | copy-start | bytes 393220
  57.2 9.3 %copy-start.2 = (f32[2,128,128]{2,1,0:T(8,128)S(1)}, f32[2,128,128]{2,1,0:T(8,128)}, u32[]{:S(2)}) copy-start(f32[2,128,128]{2,1,0:T(8,128)} %block_above.1) | copy-start | bytes 393220
  57.5 10.3 %collective-permute-start = (f32[2,32,128]{2,1,0:T(8,128)S(1)}, f32[2,32,128]{2,1,0:T(8,128)S(1)}, u32[]{:S(2)}, u32[]{:S(2)}) collective-permute-start(f32[2,32,128]{2,1,0:T(8,128)S(1)} %get-tuple-element.15), channel_id=1, source_target_pairs={{0,1},{1,2},{2,3},{3,4},{4,5},{5,6},{6,7},{8,9},{9,10},{10,11},{11... | collective-permute-start | bytes 98312 | tf_op jit(solution)/shard_map/ppermute | solution.py:355
  64.5 5.2 %collective-permute-start.1 = (f32[2,32,128]{2,1,0:T(8,128)S(1)}, f32[2,32,128]{2,1,0:T(8,128)S(1)}, u32[]{:S(2)}, u32[]{:S(2)}) collective-permute-start(f32[2,32,128]{2,1,0:T(8,128)S(1)} %get-tuple-element.16), channel_id=1, source_target_pairs={{1,0},{2,1},{3,2},{4,3},{5,4},{6,5},{7,6},{9,8},{10,9},{11,10},{12... | collective-permute-start | bytes 98312 | tf_op jit(solution)/shard_map/ppermute | solution.py:355
  66.5 0.7 copy-start.3
  66.5 0.7 copy-start.4
  94.6 10.2 %all-to-all-start.2 = ((f32[8,1,256]{2,1,0:T(1,128)}), f32[8,1,256]{2,1,0:T(1,128)S(1)}, u32[]{:S(2)}, u32[]{:S(2)}) async-start(f32[8,1,256]{2,1,0:T(1,128)} %owned.1), calls=%async_computation.2 | async-start | bytes 16384 | tf_op jit(solution)/shard_map/all_to_all | solution.py:472

commit v6 on v5

--- a/solution.py
+++ b/solution.py
@@ -82,11 +82,13 @@
             moved = jnp.where(place < ROWS, pltpu.roll(here, 1, 1), pltpu.roll(here, LANES - 1, 1))
             outer.append(jnp.where((place == 0) | (place == WIDTH - 1), v[:, span], moved))
         sides.append(outer)
-    for copy in copies[3:]:
-        copy.wait()
+
+    def send(field, level, block, cells):
+        start = block * ROWS * stride + field * levels + level
+        lines[pl.ds(start, ROWS, stride=stride), :] = to_lines(cells, row_of)
+
     for block in range(blocks):
         span = slice(block * LANES, (block + 1) * LANES)
-        start = block * ROWS * stride
         rim = jnp.zeros((ROWS, LANES), jnp.float32)
         for level in range(levels):
             low = sides[level][block]
@@ -101,17 +103,17 @@
                 high = jnp.where(lane < WIDTH, 0.0, high)
             for side, picked in enumerate((along_row(low, low_lane), along_row(high, high_lane))):
                 rim = jnp.where(row == 2 * level + side, along_lane(picked, x_of), rim)
-            sent = (
-                velocity[level, :, span],
-                base[level, :, span],
-                yielded[level, :, span].astype(jnp.float32) * YIELD_WEIGHT,
-                FINITE_STEP * (colors[level, :, span] + 1).astype(jnp.float32),
-                forcing[level, :, span],
-            )
-            for field, cells in enumerate(sent):
-                lines[pl.ds(start + field * levels + level, ROWS, stride=stride), :] = to_lines(cells, row_of)
-        rim = to_lines(rim, row_of)
-        lines[pl.ds(start + FIELDS * levels, ROWS, stride=stride), :] = rim
+            send(0, level, block, velocity[level, :, span])
+            send(1, level, block, base[level, :, span])
+            send(2, level, block, yielded[level, :, span].astype(jnp.float32) * YIELD_WEIGHT)
+        send(FIELDS, 0, block, rim)
+    for copy in copies[3:]:
+        copy.wait()
+    for block in range(blocks):
+        span = slice(block * LANES, (block + 1) * LANES)
+        for level in range(levels):
+            send(3, level, block, FINITE_STEP * (colors[level, :, span] + 1).astype(jnp.float32))
+            send(4, level, block, forcing[level, :, span])
 
 
 def spread_rows(received, stride, field, levels, store):
@@ -122,7 +124,7 @@
             store(block * ROWS * levels + level, rows)
 
 
-def edge_kernel(levels, received, velocity, viscosity, base, coef, low_edge, high_edge):
+def edge_kernel(levels, received, velocity, viscosity, base, coef, inner_edge, outer_edge):
     radial = base.shape[0]
     stride = received.shape[0] * levels // radial
     nothing = jnp.zeros((ROWS, LANES), jnp.float32)
@@ -143,14 +145,15 @@
         spread_rows(received, stride, field, levels, store)
     _, group, place = places()
     shift = lax.axis_index("lat") & (ROWS - 1)
-    first_lane = shift * WIDTH + place
-    last_lane = ((shift + ROWS - 1) & (ROWS - 1)) * WIDTH + place
+    odd = lax.axis_index("sec") & 1
+    inner_lane = ((shift + (1 - odd) * (ROWS - 1)) & (ROWS - 1)) * WIDTH + place
+    outer_lane = ((shift + odd * (ROWS - 1)) & (ROWS - 1)) * WIDTH + place
     for start in range(0, radial, ROWS):
         v = velocity[pl.ds(ROWS + start, ROWS), :]
         eta = base[pl.ds(start, ROWS), :] / (1.0 + coef[pl.ds(start, ROWS), :] * v * v)
         viscosity[pl.ds(ROWS + start, ROWS), :] = eta
         for kind, cells in enumerate((v, eta)):
-            for edge, lane_of in ((low_edge, first_lane), (high_edge, last_lane)):
+            for edge, lane_of in ((inner_edge, inner_lane), (outer_edge, outer_lane)):
                 edge[kind, pl.ds(start // ROWS, 1), :] = along_lane(along_row(cells, lane_of), group)[:1]
 
 
@@ -254,8 +257,8 @@
     velocity,
     viscosity,
     middle,
-    left,
-    right,
+    inner,
+    outer,
     blocks_high,
     blocks_low,
     lines_of,
@@ -266,13 +269,15 @@
     devices = radial // levels
     row, group, place = places()
     x = (group - lax.axis_index("lat")) & (ROWS - 1)
-    first_x, last_x = x == 0, x == ROWS - 1
     own_lane = row * WIDTH + place
 
+    odd = lax.axis_index("sec") & 1
+    inner_x, outer_x = x == (1 - odd) * (ROWS - 1), x == odd * (ROWS - 1)
+
     def side(kind, start):
-        low = along_row(jnp.broadcast_to(left[kind, pl.ds(start // ROWS, 1), :], (ROWS, LANES)), own_lane)
-        high = along_row(jnp.broadcast_to(right[kind, pl.ds(start // ROWS, 1), :], (ROWS, LANES)), own_lane)
-        return jnp.where(first_x, low, jnp.where(last_x, high, 0.0))
+        near = along_row(jnp.broadcast_to(inner[kind, pl.ds(start // ROWS, 1), :], (ROWS, LANES)), own_lane)
+        far = along_row(jnp.broadcast_to(outer[kind, pl.ds(start // ROWS, 1), :], (ROWS, LANES)), own_lane)
+        return jnp.where(inner_x, near, jnp.where(outer_x, far, 0.0))
 
     for start in range(0, radial, ROWS):
         here = pl.ds(start, ROWS)
@@ -348,11 +353,6 @@
             correction[level, :, block * LANES : (block + 1) * LANES] = along_row(
                 along_lane(lines, row_of), lane_of
             )
-
-
-def shifted(cells, axis, step):
-    count = lax.axis_size(axis)
-    return lax.ppermute(cells, axis, [(i, i + step) for i in range(count) if 0 <= i + step < count])
 
 
 def swapped(rows, parts):
@@ -436,15 +436,15 @@
     def pencil_body(*refs):
         pencil_kernel(levels, *refs)
 
-    v, eta, base, coef, low_edge, high_edge = kernel_call(
+    v, eta, base, coef, inner_edge, outer_edge = kernel_call(
         edge_body,
         [padded, padded, whole, whole, edge, edge],
         [VMEM],
         (10 * cell_count, 7 * cell_count),
         "edges",
     )(lines)
-    left = shifted(high_edge, "sec", 1)
-    right = shifted(low_edge, "sec", -1)
+    inner = lax.ppermute(inner_edge, "sec", [(i, i ^ 1) for i in range(sectors)])
+    outer = lax.ppermute(outer_edge, "sec", [(i, i + 1 if i % 2 else i - 1) for i in range(1, sectors - 1)])
     (middle,) = kernel_call(
         middle_body,
         [f32(8, radial, LANES)],
@@ -460,7 +460,7 @@
         (24 * radial * radial * LANES, 12 * radial * LANES),
         "pencil",
         [pltpu.VMEM((3, radial, LANES), jnp.float32)],
-    )(v, eta, middle, left, right, blocks_high, blocks_low, lines_of)
+    )(v, eta, middle, inner, outer, blocks_high, blocks_low, lines_of)
     improved = swapped(improved, 2)
 
     def owned_body(*refs):

time: 106 us -> 105 us (level)
  starting transfers between devices: 14.6 us -> 16.5 us
  blocking collectives: 78 us -> 76.8 us
  waiting for transfers between devices: 5.84 us -> 4.66 us
    all_to_all x1, starting transfers between devices: 5.63 us -> 7.53 us  [local(): sums = lax.all_to_all(owned, 'sec', split_axis=0, concat_axis=0, tiled=True)]
    ppermute x2, waiting for transfers between devices: 1.99 us -> 0.81 us  [the longest x1 0.81 us: local(): lax.ppermute(outer_edge, 'sec', [(i, i + 1 if i % 2 else i - 1) for i in...]
    all_to_all x2, blocking collectives: 78 us -> 76.8 us  [swapped(): taken = lax.all_to_all(sent, 'lat', split_axis=0, concat_axis=0, tiled=True)]
where the time goes in v6:
time: 105 us
  blocking collectives  76.8 us (73%)
  starting transfers between devices  16.5 us (16%)
  Pallas kernels  5.01 us (5%)
  waiting for transfers between devices  4.66 us (4%)
    all_to_all x2, blocking collectives, swapped(): taken = lax.all_to_all(sent, 'lat', split_axis=0, concat_axis=0, tiled=True)  76.8 us
    all_to_all x1, starting transfers between devices, local(): sums = lax.all_to_all(owned, 'sec', split_axis=0, concat_axis=0, tiled=True)  7.53 us
    ppermute x1, starting transfers between devices, local(): lax.ppermute(inner_edge, 'sec', [(i, i ^ 1) for i in range(sectors)])  5.85 us
    all_to_all x1, waiting for transfers between devices, local(): sums = lax.all_to_all(owned, 'sec', split_axis=0, concat_axis=0, tiled=True)  3.85 us
    ppermute x1, starting transfers between devices, local(): lax.ppermute(outer_edge, 'sec', [(i, i + 1 if i % 2 else i - 1) for i in...  3.1 us
  transfers between devices with their start and end apart: 3, of which 2 were waited for; matrix products, arithmetic and copies ran while one was open for 0% of the time, Pallas kernels for 1%

profile of v6, /device:TPU:1, one launch (start us, length us, event | category | flops | bytes accessed | tf_op | source)
XLA Modules:
  0.0 104.9 jit_solution(14830592872783825581)
XLA Ops:
  0.6 1.8 %tile.1 = f32[1344,128]{1,0:T(8,128)S(1)} custom-call(f32[4,8,1024]{2,1,0:T(8,128)} %velocity_far.1, f32[4,8,1024]{2,1,0:T(8,128)} %base_far.1, s32[4,8,1024]{2,1,0:T(8,128)} %yielded_far.1, s32[4,8,1024]{2,1,0:T(8,128)} %colors_far.1, f32[4,8,1024]{2,1,0:T(8,128)} %forcing_far.1), custom_call_target="tpu_custom_call" | custom-call | flops 1310720 | bytes 1572864 | tf_op jit(solution)/shard_map/tile/pallas_call | solution.py:405
  2.5 54.7 %all_to_all.15 = f32[64,21,1,128]{3,2,1,0:T(1,128)S(1)} all-to-all(f32[64,21,1,128]{3,2,1,0:T(1,128)S(1)} %bitcast.9), channel_id=1, replica_groups=mesh['lat'=64,'sec'=8] {'lat'}, dimensions={0} | all-to-all | bytes 1376256 | tf_op jit(solution)/shard_map/all_to_all | solution.py:361
  57.1 0.0 copy-start
  57.2 0.0 copy-start.1
  57.2 0.0 copy-start.2
  57.2 0.2 edges.1
  57.4 5.9 %collective-permute-start = (f32[2,32,128]{2,1,0:T(8,128)S(1)}, f32[2,32,128]{2,1,0:T(8,128)S(1)}, u32[]{:S(2)}, u32[]{:S(2)}) collective-permute-start(f32[2,32,128]{2,1,0:T(8,128)S(1)} %get-tuple-element.15), channel_id=1, source_target_pairs={{0,1},{1,0},{2,3},{3,2},{4,5},{5,4},{6,7},{7,6},{8,9},{9,8},{10,11... | collective-permute-start | bytes 98312 | tf_op jit(solution)/shard_map/ppermute | solution.py:446
  63.3 3.1 %collective-permute-start.1 = (f32[2,32,128]{2,1,0:T(8,128)S(1)}, f32[2,32,128]{2,1,0:T(8,128)S(1)}, u32[]{:S(2)}, u32[]{:S(2)}) collective-permute-start(f32[2,32,128]{2,1,0:T(8,128)S(1)} %get-tuple-element.16), channel_id=1, source_target_pairs={{1,2},{2,1},{3,4},{4,3},{5,6},{6,5},{9,10},{10,9},{11,12},{12,11},... | collective-permute-start | bytes 98312 | tf_op jit(solution)/shard_map/ppermute | solution.py:447
  66.4 0.0 copy-start.3
  66.4 0.0 copy-start.4
  66.4 0.0 copy-done
  66.4 0.0 copy-done.1
  66.4 0.0 copy-done.2
  66.4 0.6 copy-done.3
  67.0 0.0 copy-done.4
  67.0 0.2 lines.1
  67.2 0.5 middle.1.refs_2_
  67.7 0.0 collective-permute-done.refs_3_
  67.7 0.8 collective-permute-done.1.refs_4_
  68.5 0.9 pencil.1
  69.4 22.1 %all_to_all.16 = f32[64,3,2,128]{3,2,1,0:T(2,128)S(1)} all-to-all(f32[64,3,2,128]{3,2,1,0:T(2,128)S(1)} %bitcast.12), channel_id=1, replica_groups=mesh['lat'=64,'sec'=8] {'lat'}, dimensions={0} | all-to-all | bytes 393216 | tf_op jit(solution)/shard_map/all_to_all | solution.py:361
  91.6 0.6 owned.1
  92.2 7.5 %all-to-all-start.2 = ((f32[8,1,256]{2,1,0:T(1,128)}), f32[8,1,256]{2,1,0:T(1,128)S(1)}, u32[]{:S(2)}, u32[]{:S(2)}) async-start(f32[8,1,256]{2,1,0:T(1,128)} %owned.1), calls=%async_computation.2 | async-start | bytes 16384 | tf_op jit(solution)/shard_map/all_to_all | solution.py:472
  99.7 0.8 finish.1
  100.5 3.8 %all-to-all-done.2 = f32[8,1,256]{2,1,0:T(1,128)S(1)} async-done(((f32[8,1,256]{2,1,0:T(1,128)}), f32[8,1,256]{2,1,0:T(1,128)S(1)}, u32[]{:S(2)}, u32[]{:S(2)}) %all-to-all-start.2) | async-done | bytes 8224 | tf_op jit(solution)/shard_map/all_to_all | solution.py:472
  104.3 0.6 reduce_sum.11
Async XLA Ops:
  57.1 9.3 %copy-start = (f32[2,128,128]{2,1,0:T(8,128)S(1)}, f32[2,128,128]{2,1,0:T(8,128)}, u32[]{:S(2)}) copy-start(f32[2,128,128]{2,1,0:T(8,128)} %block_diag.1) | copy-start | bytes 393220
  57.2 9.3 %copy-start.1 = (f32[2,128,128]{2,1,0:T(8,128)S(1)}, f32[2,128,128]{2,1,0:T(8,128)}, u32[]{:S(2)}) copy-start(f32[2,128,128]{2,1,0:T(8,128)} %block_below.1) | copy-start | bytes 393220
  57.2 9.3 %copy-start.2 = (f32[2,128,128]{2,1,0:T(8,128)S(1)}, f32[2,128,128]{2,1,0:T(8,128)}, u32[]{:S(2)}) copy-start(f32[2,128,128]{2,1,0:T(8,128)} %block_above.1) | copy-start | bytes 393220
  57.4 10.3 %collective-permute-start = (f32[2,32,128]{2,1,0:T(8,128)S(1)}, f32[2,32,128]{2,1,0:T(8,128)S(1)}, u32[]{:S(2)}, u32[]{:S(2)}) collective-permute-start(f32[2,32,128]{2,1,0:T(8,128)S(1)} %get-tuple-element.15), channel_id=1, source_target_pairs={{0,1},{1,0},{2,3},{3,2},{4,5},{5,4},{6,7},{7,6},{8,9},{9,8},{10,11... | collective-permute-start | bytes 98312 | tf_op jit(solution)/shard_map/ppermute | solution.py:446
  63.3 5.2 %collective-permute-start.1 = (f32[2,32,128]{2,1,0:T(8,128)S(1)}, f32[2,32,128]{2,1,0:T(8,128)S(1)}, u32[]{:S(2)}, u32[]{:S(2)}) collective-permute-start(f32[2,32,128]{2,1,0:T(8,128)S(1)} %get-tuple-element.16), channel_id=1, source_target_pairs={{1,2},{2,1},{3,4},{4,3},{5,6},{6,5},{9,10},{10,9},{11,12},{12,11},... | collective-permute-start | bytes 98312 | tf_op jit(solution)/shard_map/ppermute | solution.py:447
  66.4 0.7 copy-start.3
  66.4 0.7 copy-start.4
  92.2 12.1 %all-to-all-start.2 = ((f32[8,1,256]{2,1,0:T(1,128)}), f32[8,1,256]{2,1,0:T(1,128)S(1)}, u32[]{:S(2)}, u32[]{:S(2)}) async-start(f32[8,1,256]{2,1,0:T(1,128)} %owned.1), calls=%async_computation.2 | async-start | bytes 16384 | tf_op jit(solution)/shard_map/all_to_all | solution.py:472

commit v7 on v6

--- a/solution.py
+++ b/solution.py
@@ -299,8 +299,8 @@
 
     def apply_blocks(field):
         high, low = halves(field)
-        small = product(blocks_high[...], low, whole) + product(blocks_low[...], high, whole)
-        return small + product(blocks_high[...], high, whole)
+        wide = product(blocks_high[...], jnp.concatenate([high, low], axis=1), whole)
+        return wide[:, :LANES] + (wide[:, LANES:] + product(blocks_low[...], high, whole))
 
     initial = apply_blocks(residual)
     level_index = lax.broadcasted_iota(jnp.int32, (radial, LANES), 0)
@@ -311,7 +311,8 @@
     gradient = correction * work[2]
     high, low = halves(gradient)
     over_lines = ((1,), (1,))
-    owned = product(lines_of[...], low, over_lines) + product(lines_of[...], high, over_lines)
+    twice = jnp.concatenate([lines_of[...], lines_of[...]], axis=1)
+    owned = product(twice, jnp.concatenate([high, low], axis=1), over_lines)
     work[0] = correction
     parts = radial // LANES
     back = levels + parts

time: 105 us -> 105 us (level)
  no operation moved by 1% of the time
where the time goes in v7:
time: 105 us
  blocking collectives  76.8 us (73%)
  starting transfers between devices  16.5 us (16%)
  Pallas kernels  4.87 us (5%)
  waiting for transfers between devices  4.66 us (4%)
    all_to_all x2, blocking collectives, swapped(): taken = lax.all_to_all(sent, 'lat', split_axis=0, concat_axis=0, tiled=True)  76.8 us
    all_to_all x1, starting transfers between devices, local(): sums = lax.all_to_all(owned, 'sec', split_axis=0, concat_axis=0, tiled=True)  7.53 us
    ppermute x1, starting transfers between devices, local(): lax.ppermute(inner_edge, 'sec', [(i, i ^ 1) for i in range(sectors)])  5.85 us
    all_to_all x1, waiting for transfers between devices, local(): sums = lax.all_to_all(owned, 'sec', split_axis=0, concat_axis=0, tiled=True)  3.85 us
    ppermute x1, starting transfers between devices, local(): lax.ppermute(outer_edge, 'sec', [(i, i + 1 if i % 2 else i - 1) for i in...  3.1 us
  transfers between devices with their start and end apart: 3, of which 2 were waited for; matrix products, arithmetic and copies ran while one was open for 0% of the time, Pallas kernels for 1%

profile of v7, /device:TPU:1, one launch (start us, length us, event | category | flops | bytes accessed | tf_op | source)
XLA Modules:
  0.0 104.8 jit_solution(14759033955900693127)
XLA Ops:
  0.6 1.8 %tile.1 = f32[1344,128]{1,0:T(8,128)S(1)} custom-call(f32[4,8,1024]{2,1,0:T(8,128)} %velocity_far.1, f32[4,8,1024]{2,1,0:T(8,128)} %base_far.1, s32[4,8,1024]{2,1,0:T(8,128)} %yielded_far.1, s32[4,8,1024]{2,1,0:T(8,128)} %colors_far.1, f32[4,8,1024]{2,1,0:T(8,128)} %forcing_far.1), custom_call_target="tpu_custom_call" | custom-call | flops 1310720 | bytes 1572864 | tf_op jit(solution)/shard_map/tile/pallas_call | solution.py:406
  2.5 54.7 %all_to_all.15 = f32[64,21,1,128]{3,2,1,0:T(1,128)S(1)} all-to-all(f32[64,21,1,128]{3,2,1,0:T(1,128)S(1)} %bitcast.9), channel_id=1, replica_groups=mesh['lat'=64,'sec'=8] {'lat'}, dimensions={0} | all-to-all | bytes 1376256 | tf_op jit(solution)/shard_map/all_to_all | solution.py:362
  57.1 0.0 copy-start
  57.2 0.0 copy-start.1
  57.2 0.0 copy-start.2
  57.2 0.2 edges.1
  57.4 5.9 %collective-permute-start = (f32[2,32,128]{2,1,0:T(8,128)S(1)}, f32[2,32,128]{2,1,0:T(8,128)S(1)}, u32[]{:S(2)}, u32[]{:S(2)}) collective-permute-start(f32[2,32,128]{2,1,0:T(8,128)S(1)} %get-tuple-element.15), channel_id=1, source_target_pairs={{0,1},{1,0},{2,3},{3,2},{4,5},{5,4},{6,7},{7,6},{8,9},{9,8},{10,11... | collective-permute-start | bytes 98312 | tf_op jit(solution)/shard_map/ppermute | solution.py:447
  63.3 3.1 %collective-permute-start.1 = (f32[2,32,128]{2,1,0:T(8,128)S(1)}, f32[2,32,128]{2,1,0:T(8,128)S(1)}, u32[]{:S(2)}, u32[]{:S(2)}) collective-permute-start(f32[2,32,128]{2,1,0:T(8,128)S(1)} %get-tuple-element.16), channel_id=1, source_target_pairs={{1,2},{2,1},{3,4},{4,3},{5,6},{6,5},{9,10},{10,9},{11,12},{12,11},... | collective-permute-start | bytes 98312 | tf_op jit(solution)/shard_map/ppermute | solution.py:448
  66.4 0.0 copy-start.3
  66.4 0.0 copy-start.4
  66.4 0.0 copy-done
  66.4 0.0 copy-done.1
  66.4 0.0 copy-done.2
  66.4 0.6 copy-done.3
  67.0 0.0 copy-done.4
  67.0 0.2 lines.1
  67.2 0.5 middle.1.refs_2_
  67.7 0.0 collective-permute-done.refs_3_
  67.7 0.8 collective-permute-done.1.refs_4_
  68.5 0.8 pencil.1
  69.3 22.1 %all_to_all.16 = f32[64,3,2,128]{3,2,1,0:T(2,128)S(1)} all-to-all(f32[64,3,2,128]{3,2,1,0:T(2,128)S(1)} %bitcast.12), channel_id=1, replica_groups=mesh['lat'=64,'sec'=8] {'lat'}, dimensions={0} | all-to-all | bytes 393216 | tf_op jit(solution)/shard_map/all_to_all | solution.py:362
  91.4 0.6 owned.1
  92.1 7.5 %all-to-all-start.2 = ((f32[8,1,256]{2,1,0:T(1,128)}), f32[8,1,256]{2,1,0:T(1,128)S(1)}, u32[]{:S(2)}, u32[]{:S(2)}) async-start(f32[8,1,256]{2,1,0:T(1,128)} %owned.1), calls=%async_computation.2 | async-start | bytes 16384 | tf_op jit(solution)/shard_map/all_to_all | solution.py:473
  99.6 0.8 finish.1
  100.4 3.8 %all-to-all-done.2 = f32[8,1,256]{2,1,0:T(1,128)S(1)} async-done(((f32[8,1,256]{2,1,0:T(1,128)}), f32[8,1,256]{2,1,0:T(1,128)S(1)}, u32[]{:S(2)}, u32[]{:S(2)}) %all-to-all-start.2) | async-done | bytes 8224 | tf_op jit(solution)/shard_map/all_to_all | solution.py:473
  104.2 0.6 reduce_sum.11
Async XLA Ops:
  57.1 9.3 %copy-start = (f32[2,128,128]{2,1,0:T(8,128)S(1)}, f32[2,128,128]{2,1,0:T(8,128)}, u32[]{:S(2)}) copy-start(f32[2,128,128]{2,1,0:T(8,128)} %block_diag.1) | copy-start | bytes 393220
  57.2 9.3 %copy-start.1 = (f32[2,128,128]{2,1,0:T(8,128)S(1)}, f32[2,128,128]{2,1,0:T(8,128)}, u32[]{:S(2)}) copy-start(f32[2,128,128]{2,1,0:T(8,128)} %block_below.1) | copy-start | bytes 393220
  57.2 9.3 %copy-start.2 = (f32[2,128,128]{2,1,0:T(8,128)S(1)}, f32[2,128,128]{2,1,0:T(8,128)}, u32[]{:S(2)}) copy-start(f32[2,128,128]{2,1,0:T(8,128)} %block_above.1) | copy-start | bytes 393220
  57.4 10.3 %collective-permute-start = (f32[2,32,128]{2,1,0:T(8,128)S(1)}, f32[2,32,128]{2,1,0:T(8,128)S(1)}, u32[]{:S(2)}, u32[]{:S(2)}) collective-permute-start(f32[2,32,128]{2,1,0:T(8,128)S(1)} %get-tuple-element.15), channel_id=1, source_target_pairs={{0,1},{1,0},{2,3},{3,2},{4,5},{5,4},{6,7},{7,6},{8,9},{9,8},{10,11... | collective-permute-start | bytes 98312 | tf_op jit(solution)/shard_map/ppermute | solution.py:447
  63.3 5.2 %collective-permute-start.1 = (f32[2,32,128]{2,1,0:T(8,128)S(1)}, f32[2,32,128]{2,1,0:T(8,128)S(1)}, u32[]{:S(2)}, u32[]{:S(2)}) collective-permute-start(f32[2,32,128]{2,1,0:T(8,128)S(1)} %get-tuple-element.16), channel_id=1, source_target_pairs={{1,2},{2,1},{3,4},{4,3},{5,6},{6,5},{9,10},{10,9},{11,12},{12,11},... | collective-permute-start | bytes 98312 | tf_op jit(solution)/shard_map/ppermute | solution.py:448
  66.4 0.7 copy-start.3
  66.4 0.7 copy-start.4
  92.1 12.1 %all-to-all-start.2 = ((f32[8,1,256]{2,1,0:T(1,128)}), f32[8,1,256]{2,1,0:T(1,128)S(1)}, u32[]{:S(2)}, u32[]{:S(2)}) async-start(f32[8,1,256]{2,1,0:T(1,128)} %owned.1), calls=%async_computation.2 | async-start | bytes 16384 | tf_op jit(solution)/shard_map/all_to_all | solution.py:473
